TPU v7x, 32 devices: a whole 2x2x4 slice. The times are simulated.
32 devices in a mesh: dp: 16 (over z, y, x), tp: 2 (over core).
Axes of the slice: x: 2, y: 2, z: 4, core: 2. Of those that a mesh axis runs over, the one named last changes fastest.
Arguments:
- tokens: bfloat16 [32768, 768], P('dp'), may hold values from -6 to 6
- segment_ids: int32 [64, 512], P('dp'), may hold values from 0 to 7, never falling along the last dimension, each value on 1 to 256 neighbouring positions
- cotangent: bfloat16 [32768, 768], P('dp'), may hold values from -6 to 6
- w_query: bfloat16 [768, 768], P('dp', 'tp'), may hold values from -0.21875 to 0.21875
- w_key: bfloat16 [768, 768], P('dp', 'tp'), may hold values from -0.21875 to 0.21875
- w_value: bfloat16 [768, 768], P('dp', 'tp'), may hold values from -0.21875 to 0.21875
- w_output: bfloat16 [768, 768], P('tp', 'dp'), may hold values from -1.75 to 1.75
- shared_down: bfloat16 [768, 1024], P('dp'), may hold values from -0.21875 to 0.21875
- shared_up: bfloat16 [1024, 768], P('dp', 'tp'), may hold values from -0.1875 to 0.1875
- w_in: bfloat16 [768, 3072], P('dp', 'tp'), may hold values from -0.21875 to 0.21875
- w_out: bfloat16 [3072, 768], P('tp', 'dp'), may hold values from -0.109375 to 0.109375
- gain_one: float32 [768], replicated, may hold values from 0.25 to 1.75
- gain_two: float32 [768], replicated, may hold values from 0.25 to 1.75
- query_scale: float32 [1024], replicated, may hold values from 0.25 to 1.25
- query_bias: float32 [768], replicated, may hold values from -1 to 1
- value_scale: float32 [1024], replicated, may hold values from 0.25 to 1.25
- value_bias: float32 [768], replicated, may hold values from -1 to 1
Outputs:
- output: bfloat16 [32768, 768], P(('dp', 'tp'))
- token_grad: float32 [32768, 768], P(('dp', 'tp'))
- query_scale_grad: float32 [1024], replicated
- query_bias_grad: float32 [768], replicated
- value_scale_grad: float32 [1024], replicated
- value_bias_grad: float32 [768], replicated
Inputs may be any that keep to these rules, and one draw needn't show every extreme that they name: `segment_ids`: within each sequence of 512 tokens the ids never fall; one sentence spans 1 to 256 tokens, and some sentence spans exactly 256.
All inputs are finite; a program needn't handle non-finite values.
Results may differ from a plain program's by a relative error of at most 0.018.
Values may be sent and summed in bfloat16 or wider, within the bound.
A program may use at most 192 MiB of HBM per device.

v0:
```python
import math

import jax
import jax.numpy as jnp
from jax import lax
from jax.sharding import PartitionSpec as P

HD = 64
SEQ_LEN = 512


def normalize(values):
    average = jnp.mean(values, axis=-1, keepdims=True)
    centered = values - average
    variance = jnp.mean(centered * centered, axis=-1, keepdims=True)
    inverse = lax.rsqrt(variance + 1e-05)
    return (centered * inverse, inverse)


def norm_back(upstream, normed, inverse, gain):
    scaled = upstream * gain
    first = jnp.mean(scaled, axis=-1, keepdims=True)
    second = jnp.mean(scaled * normed, axis=-1, keepdims=True)
    return inverse * (scaled - first - normed * second)


def times_transposed(left, right):
    return lax.dot_general(
        left, right, (((1,), (1,)), ((), ())), preferred_element_type=jnp.float32
    )


def exact_gelu(values):
    return jax.nn.gelu(values, approximate=False)


def masked_scores(queries, keys, segments):
    raw = jnp.einsum("qhe,khe->hqk", queries, keys, preferred_element_type=jnp.float32) * (
        1.0 / math.sqrt(HD)
    )
    same = segments[:, None] == segments[None, :]
    return jnp.where(same[None, :, :], raw, -1000000000.0)


def attend_forward(parts):
    queries, keys, values, segments = parts
    scores = masked_scores(queries, keys, segments)
    top = jnp.max(scores, axis=-1, keepdims=True)
    powers = jnp.exp(scores - top)
    total = jnp.sum(powers, axis=-1, keepdims=True)
    weights_low = (powers / total).astype(jnp.bfloat16)
    mixed = jnp.einsum(
        "hqk,khe->qhe", weights_low, values, preferred_element_type=jnp.float32
    ).astype(jnp.bfloat16)
    return (mixed, (top + jnp.log(total))[:, :, 0])


def attend_backward(parts):
    queries, keys, values, segments, logsum, mixed_grad = parts
    scores = masked_scores(queries, keys, segments)
    probs = jnp.exp(scores - logsum[:, :, None])
    weights_low = probs.astype(jnp.bfloat16)
    value_grad = jnp.einsum(
        "hqk,qhe->khe", weights_low, mixed_grad, preferred_element_type=jnp.float32
    ).astype(jnp.bfloat16)
    prob_grad = jnp.einsum("qhe,khe->hqk", mixed_grad, values, preferred_element_type=jnp.float32)
    score_grad = (probs * (prob_grad - jnp.sum(probs * prob_grad, axis=-1, keepdims=True))).astype(
        jnp.bfloat16
    )
    factor = 1.0 / math.sqrt(HD)
    query_grad = (
        jnp.einsum("hqk,khe->qhe", score_grad, keys, preferred_element_type=jnp.float32) * factor
    ).astype(jnp.bfloat16)
    key_grad = (
        jnp.einsum("hqk,qhe->khe", score_grad, queries, preferred_element_type=jnp.float32) * factor
    ).astype(jnp.bfloat16)
    return (query_grad, key_grad, value_grad)


def per_device(
    tokens,
    segment_ids,
    cotangent,
    w_query,
    w_key,
    w_value,
    w_output,
    shared_down,
    shared_up,
    w_in,
    w_out,
    gain_one,
    gain_two,
    query_scale,
    query_bias,
    value_scale,
    value_bias,
):
    cores = lax.axis_size("tp")
    core = lax.axis_index("tp")
    half_rows = tokens.shape[0] // cores
    query_full, key_full, value_full, output_full, down_full, up_full = (
        lax.all_gather(w_query, "dp", axis=0, tiled=True),
        lax.all_gather(w_key, "dp", axis=0, tiled=True),
        lax.all_gather(w_value, "dp", axis=0, tiled=True),
        lax.all_gather(w_output, "dp", axis=1, tiled=True),
        lax.all_gather(shared_down, "dp", axis=0, tiled=True),
        lax.all_gather(shared_up, "dp", axis=0, tiled=True),
    )
    offset = core * query_full.shape[1]
    rows = tokens.shape[0]
    sequences = segment_ids.shape[0]
    local_width = query_full.shape[1]
    local_heads = local_width // HD
    query_bias_local = lax.dynamic_slice_in_dim(query_bias, offset, local_width)
    value_bias_local = lax.dynamic_slice_in_dim(value_bias, offset, local_width)
    projected = jnp.dot(tokens, down_full, preferred_element_type=jnp.float32)
    query_low = (projected * query_scale).astype(jnp.bfloat16)
    value_low = (projected * value_scale).astype(jnp.bfloat16)
    query_delta = jnp.dot(query_low, up_full, preferred_element_type=jnp.float32)
    value_delta = jnp.dot(value_low, up_full, preferred_element_type=jnp.float32)
    queries = (
        jnp.dot(tokens, query_full, preferred_element_type=jnp.float32)
        + query_bias_local * query_delta
    ).astype(jnp.bfloat16)
    keys = jnp.dot(tokens, key_full, preferred_element_type=jnp.float32).astype(jnp.bfloat16)
    values = (
        jnp.dot(tokens, value_full, preferred_element_type=jnp.float32)
        + value_bias_local * value_delta
    ).astype(jnp.bfloat16)
    split = (sequences, SEQ_LEN, local_heads, HD)
    query_blocks = queries.reshape(split)
    key_blocks = keys.reshape(split)
    value_blocks = values.reshape(split)
    mixed, logsum = lax.map(attend_forward, (query_blocks, key_blocks, value_blocks, segment_ids))
    mixed = mixed.reshape(rows, local_width)
    attention_part = jnp.dot(mixed, output_full, preferred_element_type=jnp.float32)
    attention = lax.psum(attention_part, "tp")
    normed_one, inverse_one = normalize(tokens.astype(jnp.float32) + attention)
    hidden = normed_one * gain_one
    hidden_low = hidden.astype(jnp.bfloat16)
    in_full, out_full = (
        lax.all_gather(w_in, "dp", axis=0, tiled=True),
        lax.all_gather(w_out, "dp", axis=1, tiled=True),
    )
    activation = jnp.dot(hidden_low, in_full, preferred_element_type=jnp.float32)
    inner, gelu_back = jax.vjp(exact_gelu, activation)
    inner_low = inner.astype(jnp.bfloat16)
    branch_part = jnp.dot(inner_low, out_full, preferred_element_type=jnp.float32)
    branch = lax.psum(branch_part.astype(jnp.bfloat16), "tp").astype(jnp.float32)
    normed_two, inverse_two = normalize(hidden + branch)
    output = (normed_two * gain_two).astype(jnp.bfloat16)
    query_back, key_back, value_back, output_back, down_back, up_back = (
        lax.all_gather(w_query, "dp", axis=0, tiled=True),
        lax.all_gather(w_key, "dp", axis=0, tiled=True),
        lax.all_gather(w_value, "dp", axis=0, tiled=True),
        lax.all_gather(w_output, "dp", axis=1, tiled=True),
        lax.all_gather(shared_down, "dp", axis=0, tiled=True),
        lax.all_gather(shared_up, "dp", axis=0, tiled=True),
    )
    in_back, out_back = (
        lax.all_gather(w_in, "dp", axis=0, tiled=True),
        lax.all_gather(w_out, "dp", axis=1, tiled=True),
    )
    sum_two_grad = norm_back(cotangent.astype(jnp.float32), normed_two, inverse_two, gain_two)
    branch_grad = sum_two_grad.astype(jnp.bfloat16)
    inner_grad = times_transposed(branch_grad, out_back)
    (activation_grad,) = gelu_back(inner_grad)
    activation_low = activation_grad.astype(jnp.bfloat16)
    feed_back_part = times_transposed(activation_low, in_back)
    hidden_grad = sum_two_grad + lax.psum(feed_back_part.astype(jnp.bfloat16), "tp").astype(
        jnp.float32
    )
    sum_one_grad = norm_back(hidden_grad, normed_one, inverse_one, gain_one)
    attention_grad = sum_one_grad.astype(jnp.bfloat16)
    mixed_grad = times_transposed(attention_grad, output_back).astype(jnp.bfloat16)
    query_grad, key_grad, value_grad = lax.map(
        attend_backward,
        (query_blocks, key_blocks, value_blocks, segment_ids, logsum, mixed_grad.reshape(split)),
    )
    query_grad = query_grad.reshape(rows, local_width)
    key_grad = key_grad.reshape(rows, local_width)
    value_grad = value_grad.reshape(rows, local_width)
    query_grad_wide = query_grad.astype(jnp.float32)
    value_grad_wide = value_grad.astype(jnp.float32)
    query_bias_part = jnp.sum(query_grad_wide * query_delta, axis=0)
    value_bias_part = jnp.sum(value_grad_wide * value_delta, axis=0)
    query_delta_grad = (query_grad_wide * query_bias_local).astype(jnp.bfloat16)
    value_delta_grad = (value_grad_wide * value_bias_local).astype(jnp.bfloat16)
    query_low_grad = times_transposed(query_delta_grad, up_back)
    value_low_grad = times_transposed(value_delta_grad, up_back)
    query_scale_part = jnp.sum(projected * query_low_grad, axis=0)
    value_scale_part = jnp.sum(projected * value_low_grad, axis=0)
    projected_terms = query_low_grad * query_scale + value_low_grad * value_scale
    token_terms = times_transposed(query_grad, query_back) + times_transposed(key_grad, key_back)
    token_terms = token_terms + times_transposed(value_grad, value_back)
    projected_grad = lax.psum_scatter(
        projected_terms.astype(jnp.bfloat16), "tp", scatter_dimension=1, tiled=True
    )
    share = projected_grad.shape[1]
    down_share = lax.dynamic_slice_in_dim(down_back, core * share, share, 1)
    token_terms = token_terms + times_transposed(projected_grad, down_share)
    token_grad = sum_one_grad + lax.psum(token_terms.astype(jnp.bfloat16), "tp").astype(jnp.float32)
    output = lax.dynamic_slice_in_dim(output, core * half_rows, half_rows, 0)
    token_grad = lax.dynamic_slice_in_dim(token_grad, core * half_rows, half_rows, 0)
    width = query_bias.shape[0]
    query_bias_spread = lax.dynamic_update_slice_in_dim(
        jnp.zeros((width,), jnp.float32), query_bias_part, offset, 0
    )
    value_bias_spread = lax.dynamic_update_slice_in_dim(
        jnp.zeros((width,), jnp.float32), value_bias_part, offset, 0
    )
    query_scale_grad, query_bias_grad, value_scale_grad, value_bias_grad = lax.psum(
        (query_scale_part, query_bias_spread, value_scale_part, value_bias_spread), ("dp", "tp")
    )
    return (
        output,
        token_grad,
        query_scale_grad,
        query_bias_grad,
        value_scale_grad,
        value_bias_grad,
    )


def solution(mesh):
    in_specs = (
        P("dp", None),
        P("dp", None),
        P("dp", None),
        P("dp", "tp"),
        P("dp", "tp"),
        P("dp", "tp"),
        P("tp", "dp"),
        P("dp", None),
        P("dp", "tp"),
        P("dp", "tp"),
        P("tp", "dp"),
        P(),
        P(),
        P(),
        P(),
        P(),
        P(),
    )
    out_specs = (P(("dp", "tp"), None), P(("dp", "tp"), None), P(), P(), P(), P())
    return jax.shard_map(
        per_device, mesh=mesh, in_specs=in_specs, out_specs=out_specs, check_vma=False
    )
```

profile of v0, /device:TPU:0, one launch (start us, length us, event | category | flops | bytes accessed | tf_op | source)
XLA Modules:
  0.0 777.9 jit_solution(16942765481318295072)
XLA Ops:
  9.5 47.0 %all_gather.36 = bf16[768,384]{1,0:T(8,128)(2,1)S(1)} all-gather(bf16[48,384]{1,0:T(8,128)(2,1)} %param.25), channel_id=1, replica_groups=mesh['dp'=16,'tp'=2] {'dp'}, dimensions={0}, use_global_device_ids=true | all-gather | bytes 626688 | tf_op jit(solution)/shard_map/all_gather | solution.py:104
  57.3 3.7 convolution_convert_fusion
  63.3 40.0 %all_gather.32 = bf16[768,384]{1,0:T(8,128)(2,1)S(1)} all-gather(bf16[48,384]{1,0:T(8,128)(2,1)S(1)} %copy-done.33), channel_id=1, replica_groups=mesh['dp'=16,'tp'=2] {'dp'}, dimensions={0}, use_global_device_ids=true | all-gather | bytes 626688 | tf_op jit(solution)/shard_map/all_gather | solution.py:105
  103.3 41.5 %all_gather.35 = bf16[768,384]{1,0:T(8,128)(2,1)S(1)} all-gather(bf16[48,384]{1,0:T(8,128)(2,1)} %param.24), channel_id=1, replica_groups=mesh['dp'=16,'tp'=2] {'dp'}, dimensions={0}, use_global_device_ids=true | all-gather | bytes 626688 | tf_op jit(solution)/shard_map/all_gather | solution.py:103
  144.8 42.1 %all_gather.37 = bf16[384,768]{0,1:T(8,128)(2,1)} all-gather(bf16[384,48]{0,1:T(8,128)(2,1)} %param.27), channel_id=1, replica_groups=mesh['dp'=16,'tp'=2] {'dp'}, dimensions={1}, use_global_device_ids=true | all-gather | bytes 626688 | tf_op jit(solution)/shard_map/all_gather | solution.py:106
  186.8 41.7 %all_gather.34 = bf16[1024,384]{1,0:T(8,128)(2,1)S(1)} all-gather(bf16[64,384]{1,0:T(8,128)(2,1)} %param.29), channel_id=1, replica_groups=mesh['dp'=16,'tp'=2] {'dp'}, dimensions={0}, use_global_device_ids=true | all-gather | bytes 835584 | tf_op jit(solution)/shard_map/all_gather | solution.py:108
  228.6 6.1 fusion.107
  246.0 3.8 reshape.170
  252.8 5.9 fusion.69
  270.4 31.3 %while.26 = (s32[]{:T(128)}, bf16[4,512,6,64]{1,3,2,0:T(8,128)(2,1)}, f32[4,6,512]{2,1,0:T(8,128)}, bf16[4,512,6,64]{1,3,2,0:T(8,128)(2,1)}, s32[4,512]{1,0:T(4,...) while((s32[]{:T(128)}, bf16[4,512,6,64]{1,3,2,0:T(8,128)(2,1)}, ...), condition=%wide.region_3.4_spmd, body=%wide.region_0.3_spmd.sunk | while | flops 421983232 | bytes 21606500 | solution.py:135
  273.9 3.7 fusion.158
  281.6 3.7 fusion.158
  289.4 3.7 fusion.158
  297.2 3.7 fusion.158
  301.7 3.8 copy.46
  305.9 4.4 fusion.108
  311.8 26.8 %all-reduce.6.cloned.1.call-done = f32[2048,768]{1,0:T(8,128)} async-done(((f32[2048,768]{1,0:T(8,128)}), f32[2048,768]{1,0:T(8,128)}) %all-reduce.6.cloned.1.call-update) | async-done | bytes 6291472 | tf_op jit(solution)/shard_map/psum | solution.py:138
  338.6 3.5 fusion.106
  345.5 59.8 %all-gather.6.cloned.1.call-done = bf16[768,1536]{1,0:T(8,128)(2,1)} async-done(((bf16[48,1536]{1,0:T(8,128)(2,1)}), bf16[768,1536]{1,0:T(8,128)(2,1)}) %all-gather.6.cloned.1.call-update) | async-done | bytes 2359312 | tf_op jit(solution)/shard_map/all_gather | solution.py:143
  405.3 34.5 %fusion.59 = (f32[2048,1536]{1,0:T(8,128)}, f32[2048,1536]{1,0:T(8,128)}) fusion(bf16[768,1536]{1,0:T(8,128)(2,1)} %all-gather.6.cloned.1.call-done, f32[2048,768]{1,0:T(8,128)} %copy-done, f32[768]{0:T(1024)S(1)} %copy-done.32, f32[2048]{0:T(1024)S(1)} %add_rsqrt_fusion.1, f32[2048]{0:T(1024)S(1)} %broadcast_multiply_fusion.5), kind=kOutput, calls=%fused_computation.67 | convolution fusion | flops 5033164800 | bytes 33836032 | tf_op jit(solution)/shard_map/dot_general | solution.py:146
  439.8 29.7 %all-gather.8.cloned.1.call-done = bf16[1536,768]{0,1:T(8,128)(2,1)} async-done(((bf16[1536,48]{0,1:T(8,128)(2,1)}), bf16[1536,768]{0,1:T(8,128)(2,1)}) %all-gather.8.cloned.1.call-update) | async-done | bytes 2359312 | tf_op jit(solution)/shard_map/all_gather | solution.py:144
  469.5 12.6 %fusion.73 = bf16[2048,768]{1,0:T(8,128)(2,1)} fusion(bf16[1536,768]{0,1:T(8,128)(2,1)} %all-gather.8.cloned.1.call-done, f32[2048,1536]{1,0:T(8,128)} %get-tuple-element.189, f32[2048,1536]{1,0:T(8,128)} %get-tuple-element.190), kind=kOutput, calls=%fused_computation.114 | convolution fusion | flops 4842848256 | bytes 30670848 | tf_op jit(solution)/shard_map/dot_general | solution.py:149
  482.3 22.1 %all-reduce.8.cloned.1.call-done = bf16[2048,768]{1,0:T(8,128)(2,1)} async-done(((bf16[2048,768]{1,0:T(8,128)(2,1)}), bf16[2048,768]{1,0:T(8,128)(2,1)}) %all-reduce.8.cloned.1.call-update) | async-done | bytes 3145744 | tf_op jit(solution)/shard_map/psum | solution.py:150
  504.4 5.2 fusion.105
  509.7 4.3 multiply_reduce_fusion.5
  514.1 4.0 fusion.66
  520.8 3.3 subtract_multiply_fusion.1
  524.1 20.2 %fusion.74 = bf16[2048,768]{1,0:T(8,128)(2,1)} fusion(bf16[768,1536]{1,0:T(8,128)(2,1)S(1)} %copy-done.44, f32[2048,1536]{1,0:T(8,128)} %get-tuple-element.189, f32[2048,1536]{1,0:T(8,128)} %get-tuple-element.190, bf16[1536,768]{0,1:T(8,128)(2,1)} %all-gather.8.cloned.1.call-done, f32[2048,768]{1,0:T(8,128)} %subtract_multiply_fusion.1), kind=kOutput, calls=%fused_computation.115 | convolution fusion | flops 9710862336 | bytes 39321600 | tf_op jit(solution)/shard_map/dot_general | solution.py:28
  544.4 24.5 %all-reduce.10.cloned.1.call-done = bf16[2048,768]{1,0:T(8,128)(2,1)} async-done(((bf16[2048,768]{1,0:T(8,128)(2,1)}), bf16[2048,768]{1,0:T(8,128)(2,1)}) %all-reduce.10.cloned.1.call-update) | async-done | bytes 3145744 | tf_op jit(solution)/shard_map/psum | solution.py:171
  568.9 6.9 fusion.91
  575.8 6.2 subtract_multiply_fusion
  588.2 4.0 reshape.174
  597.8 68.2 %while.27 = (s32[]{:T(128)}, bf16[4,512,6,64]{1,3,2,0:T(8,128)(2,1)}, bf16[4,512,6,64]{1,3,2,0:T(8,128)(2,1)}, bf16[4,512,6,64]{1,3,2,0:T(8,128)(2,1)}, bf16[4,5...) while((s32[]{:T(128)}, ...), condition=%wide.region_17.18_spmd, body=%wide.region_15.17_spmd.sunk | while | flops 1031468032 | bytes 64851124 | solution.py:177
  601.9 3.2 multiply_reduce_fusion.8
  611.3 3.7 fusion.170
  628.3 3.7 fusion.170
  635.9 3.2 multiply_reduce_fusion.8
  645.3 3.7 fusion.170
  662.3 3.7 fusion.170
  671.0 7.2 fusion.94
  683.5 9.9 %multiply_reduce_fusion.1 = (f32[1024]{0:T(1024)S(1)}, f32[1024]{0:T(1024)S(1)}, bf16[2048,1024]{1,0:T(8,128)(2,1)}) fusion(f32[2048,1024]{1,0:T(8,128)} %copy-done.1, f32[2048,1024]{1,0:T(8,128)} %fusion.94, f32[1024]{0:T(1024)S(1)} %copy-done.37, f32[1024]{0:T(1024)S(1)} %copy-done.39, bf16[1024,384]{1,0:T(8,128)(2,1)S(1)} %copy-done.10, ...), kind=kOutput, calls=%fused_computation.83 | convolution fusion | flops 1629747200 | bytes 23348736 | tf_op jit(solution)/shard_map/dot_general | solution.py:28
  696.9 4.6 fusion.109
  701.5 4.7 fusion.110
  706.9 3.8 fusion.98
  710.8 7.0 add_convert_fusion.2
  717.8 3.4 fusion.80
  725.5 40.8 %all-reduce = (f32[1024]{0:T(1024)}, f32[768]{0:T(1024)}, f32[1024]{0:T(1024)}, f32[768]{0:T(1024)}) all-reduce(f32[1024]{0:T(1024)S(1)} %get-tuple-element.140, f32[768]{0:T(1024)S(1)} %dynamic_update_slice.23, f32[1024]{0:T(1024)S(1)} %get-tuple-element.139, ...), channel_id=1, replica_groups=mesh['dp'=16,'tp'=2] {'dp','tp'}, use_global_device_ids=true, to_apply=%region_21.22 | all-reduce | flops 3584 | bytes 28672 | tf_op jit(solution)/shard_map/psum | solution.py:213
  766.3 4.3 dynamic-slice_add_fusion
  (220 shorter events, 132.8 us)
Async XLA Ops:
  7.2 221.4 %all-gather.4.cloned.1.call-start = ((), (), s32[]{:S(2)}) async-start(), calls=%async_computation.1 | async-start | bytes 1671168 | tf_op jit(solution)/shard_map/all_gather | solution.py:107
  7.9 330.7 %all-reduce.6.cloned.1.call-start = ((), (), s32[]{:S(2)}) async-start(), calls=%async_computation.2 | async-start | bytes 12582912 | tf_op jit(solution)/shard_map/psum | solution.py:138
  8.7 228.3 %copy-start.42 = (f32[384]{0:T(512)}, f32[384]{0:T(512)S(1)}, u32[]{:S(2)}) copy-start(f32[384]{0:T(512)S(1)} %dynamic_slice.48) | copy-start | bytes 4612
  9.5 249.1 %copy-start.40 = (f32[384]{0:T(512)}, f32[384]{0:T(512)S(1)}, u32[]{:S(2)}) copy-start(f32[384]{0:T(512)S(1)} %dynamic_slice.49) | copy-start | bytes 4612
  103.3 133.8 %copy-start.26 = (bf16[768,384]{1,0:T(8,128)(2,1)}, bf16[768,384]{1,0:T(8,128)(2,1)S(1)}, u32[]{:S(2)}) copy-start(bf16[768,384]{1,0:T(8,128)(2,1)S(1)} %all_gather.32) | copy-start | bytes 1769476
  144.7 113.9 %copy-start.30 = (bf16[768,384]{1,0:T(8,128)(2,1)}, bf16[768,384]{1,0:T(8,128)(2,1)S(1)}, u32[]{:S(2)}) copy-start(bf16[768,384]{1,0:T(8,128)(2,1)S(1)} %all_gather.35) | copy-start | bytes 1769476
  228.6 24.2 %copy-start.9 = (bf16[1024,384]{1,0:T(8,128)(2,1)}, bf16[1024,384]{1,0:T(8,128)(2,1)S(1)}, u32[]{:S(2)}) copy-start(bf16[1024,384]{1,0:T(8,128)(2,1)S(1)} %all_gather.34) | copy-start | bytes 2359300
  228.6 6.1 copy-start.36
  234.7 3.9 copy-start.1
  234.7 5.6 copy-start.23
  243.2 9.5 %copy-start.38 = (f32[1024]{0:T(1024)S(1)}, f32[1024]{0:T(1024)}, u32[]{:S(2)}) copy-start(f32[1024]{0:T(1024)} %param.34) | copy-start | bytes 12292
  252.7 7.6 copy-start.24
  301.7 8.7 %copy-start.5 = (bf16[4,512,6,64]{1,3,2,0:T(8,128)(2,1)}, bf16[4,512,6,64]{1,3,2,0:T(8,128)(2,1)S(1)}, u32[]{:S(2)}) copy-start(bf16[4,512,6,64]{1,3,2,0:T(8,128)(2,1)S(1)} %get-tuple-element.372) | copy-start | bytes 4718596
  301.7 8.7 %copy-start.7 = (bf16[4,512,6,64]{1,3,2,0:T(8,128)(2,1)}, bf16[4,512,6,64]{1,3,2,0:T(8,128)(2,1)S(1)}, u32[]{:S(2)}) copy-start(bf16[4,512,6,64]{1,3,2,0:T(8,128)(2,1)S(1)} %get-tuple-element.373) | copy-start | bytes 4718596
  301.7 4.2 copy-start.21
  310.4 28.2 %copy-start.25 = (bf16[2048,768]{1,0:T(8,128)(2,1)S(1)}, bf16[2048,768]{1,0:T(8,128)(2,1)}, u32[]{:S(2)}) copy-start(bf16[2048,768]{1,0:T(8,128)(2,1)} %param.21) | copy-start | bytes 9437188
  310.4 94.9 %all-gather.6.cloned.1.call-start = ((), (), s32[]{:S(2)}) async-start(), calls=%async_computation.3 | async-start | bytes 2506752 | tf_op jit(solution)/shard_map/all_gather | solution.py:143
  311.2 158.4 %all-gather.8.cloned.1.call-start = ((), (), s32[]{:S(2)}) async-start(), calls=%async_computation.4 | async-start | bytes 2506752 | tf_op jit(solution)/shard_map/all_gather | solution.py:144
  311.7 192.6 %all-reduce.8.cloned.1.call-start = ((), (), s32[]{:S(2)}) async-start(), calls=%async_computation.5 | async-start | bytes 6291456 | tf_op jit(solution)/shard_map/psum | solution.py:150
  342.1 63.2 %copy-start.32 = (f32[768]{0:T(1024)S(1)}, f32[768]{0:T(1024)}, u32[]{:S(2)}) copy-start(f32[768]{0:T(1024)} %param.32) | copy-start | bytes 9220
  482.2 86.7 %all-reduce.10.cloned.1.call-start = ((), (), s32[]{:S(2)}) async-start(), calls=%async_computation.6 | async-start | bytes 6291456 | tf_op jit(solution)/shard_map/psum | solution.py:171
  504.4 5.3 copy-start.8
  504.4 9.6 %slice-start = ((s8[6291456]{0:T(1024)(128)(4,1)}), s8[4194304]{0:T(1024)(128)(4,1)S(1)}, s32[]{:S(2)}) async-start(s8[6291456]{0:T(1024)(128)(4,1)} %bitcast.161), calls=%async_computation.9 | async-start | bytes 8388608
  509.6 4.4 copy-start.16
  509.6 4.4 copy-start.34
  509.7 4.5 slice-start.1
  544.3 162.6 %reduce-scatter.2.cloned.1.call-start = ((), (), s32[]{:S(2)}) async-start(), calls=%async_computation.7 | async-start | bytes 6291456 | tf_op jit(solution)/shard_map/reduce_scatter | solution.py:197
  568.9 6.9 copy-start.17
  575.8 8.9 %copy-start.22 = (bf16[384,768]{0,1:T(8,128)(2,1)S(1)}, bf16[384,768]{0,1:T(8,128)(2,1)}, u32[]{:S(2)}) copy-start(bf16[384,768]{0,1:T(8,128)(2,1)} %all_gather.37) | copy-start | bytes 1769476
  588.1 9.6 %copy-start.6 = (bf16[4,512,6,64]{1,3,2,0:T(8,128)(2,1)S(1)}, bf16[4,512,6,64]{1,3,2,0:T(8,128)(2,1)}, u32[]{:S(2)}) copy-start(bf16[4,512,6,64]{1,3,2,0:T(8,128)(2,1)} %copy-done.5) | copy-start | bytes 4718596
  597.9 7.2 copy-start.18
  611.3 3.7 copy-start.19
  615.0 7.2 copy-start.18
  632.0 7.2 copy-start.18
  649.0 7.2 copy-start.18
  666.0 4.9 copy-start.10
  666.0 4.9 copy-start.41
  671.0 7.2 copy-start.20
  678.1 5.4 copy-start.37
  678.1 5.4 copy-start.39
  678.1 5.4 copy-start.43
  693.5 72.8 %all-reduce.12.cloned.1.call-start = ((), (), s32[]{:S(2)}) async-start(), calls=%async_computation.8 | async-start | bytes 6291456 | tf_op jit(solution)/shard_map/psum | solution.py:203
  696.9 4.6 copy-start.29
  706.2 4.4 copy-start.15
  706.2 4.4 copy-start.27
  706.9 3.9 copy-start.4
  710.8 7.0 copy-start.35
  717.8 5.6 copy-start.12
  (13 other events, 35.6 us)
Sparse Core Ops, SparseCore 0:
  10.8 63.0 all-gather.3
  310.5 28.0 all-reduce.5
  341.8 63.4 all-gather.5
  408.4 61.1 all-gather.7
  482.3 22.0 all-reduce.7
  544.5 24.3 all-reduce.9
  693.6 13.2 reduce-scatter.1
  717.9 24.3 all-reduce.11
where the time goes:
time: 787 us; the launch traced here: 778 us
  blocking collectives  253 us (32%)
  matrix products  208 us (26%)
  waiting for transfers between devices  166 us (21%)
  local copies, waits for them, and re-layouts  72.1 us (9%)
  other arithmetic  62.9 us (8%)
  between operations  15.2 us (2%)
    all_gather x1, waiting for transfers between devices, per_device(): lax.all_gather(w_in, 'dp', axis=0, tiled=True)  59.8 us
    dot_general x8, matrix products, times_transposed(): lax.dot_general(left, right, (((1,), (1,)), ((), ())), preferred_element_...  59.2 us
    all_gather x1, blocking collectives, per_device(): lax.all_gather(w_key, 'dp', axis=0, tiled=True)  47 us
    all_gather x1, blocking collectives, per_device(): lax.all_gather(w_output, 'dp', axis=1, tiled=True)  42.1 us
    all_gather x1, blocking collectives, per_device(): lax.all_gather(shared_up, 'dp', axis=0, tiled=True)  41.7 us
    all_gather x1, blocking collectives, per_device(): lax.all_gather(w_query, 'dp', axis=0, tiled=True)  41.5 us
    psum x1, blocking collectives, per_device(): lax.psum((query_scale_part, query_bias_spread, value_scale_part, value_bi...  40.8 us
    all_gather x1, blocking collectives, per_device(): lax.all_gather(w_value, 'dp', axis=0, tiled=True)  40 us
  transfers between devices with their start and end apart: 8, of which 6 were waited for; matrix products, arithmetic and copies ran while one was open for 9% of the time, Pallas kernels for 0%

commit v1 on v0

v1 whole, which is shorter than its diff:
```python
import functools
import math

import jax
import jax.numpy as jnp
from jax import lax
from jax.experimental import pallas as pl
from jax.experimental.pallas import tpu as pltpu
from jax.sharding import PartitionSpec as P

HD = 64
SEQ_LEN = 512
TILE_ROWS = 16
MESH = pl.DeviceIdType.MESH


def normalize(values):
    average = jnp.mean(values, axis=-1, keepdims=True)
    centered = values - average
    variance = jnp.mean(centered * centered, axis=-1, keepdims=True)
    inverse = lax.rsqrt(variance + 1e-05)
    return (centered * inverse, inverse)


def norm_back(upstream, normed, inverse, gain):
    scaled = upstream * gain
    first = jnp.mean(scaled, axis=-1, keepdims=True)
    second = jnp.mean(scaled * normed, axis=-1, keepdims=True)
    return inverse * (scaled - first - normed * second)


def times_transposed(left, right):
    return lax.dot_general(
        left, right, (((1,), (1,)), ((), ())), preferred_element_type=jnp.float32
    )


def exact_gelu(values):
    return jax.nn.gelu(values, approximate=False)


def masked_scores(queries, keys, segments):
    raw = jnp.einsum("qhe,khe->hqk", queries, keys, preferred_element_type=jnp.float32) * (
        1.0 / math.sqrt(HD)
    )
    same = segments[:, None] == segments[None, :]
    return jnp.where(same[None, :, :], raw, -1000000000.0)


def attend_forward(parts):
    queries, keys, values, segments = parts
    scores = masked_scores(queries, keys, segments)
    top = jnp.max(scores, axis=-1, keepdims=True)
    powers = jnp.exp(scores - top)
    total = jnp.sum(powers, axis=-1, keepdims=True)
    weights_low = (powers / total).astype(jnp.bfloat16)
    mixed = jnp.einsum(
        "hqk,khe->qhe", weights_low, values, preferred_element_type=jnp.float32
    ).astype(jnp.bfloat16)
    return (mixed, (top + jnp.log(total))[:, :, 0])


def attend_backward(parts):
    queries, keys, values, segments, logsum, mixed_grad = parts
    scores = masked_scores(queries, keys, segments)
    probs = jnp.exp(scores - logsum[:, :, None])
    weights_low = probs.astype(jnp.bfloat16)
    value_grad = jnp.einsum(
        "hqk,qhe->khe", weights_low, mixed_grad, preferred_element_type=jnp.float32
    ).astype(jnp.bfloat16)
    prob_grad = jnp.einsum("qhe,khe->hqk", mixed_grad, values, preferred_element_type=jnp.float32)
    score_grad = (probs * (prob_grad - jnp.sum(probs * prob_grad, axis=-1, keepdims=True))).astype(
        jnp.bfloat16
    )
    factor = 1.0 / math.sqrt(HD)
    query_grad = (
        jnp.einsum("hqk,khe->qhe", score_grad, keys, preferred_element_type=jnp.float32) * factor
    ).astype(jnp.bfloat16)
    key_grad = (
        jnp.einsum("hqk,qhe->khe", score_grad, queries, preferred_element_type=jnp.float32) * factor
    ).astype(jnp.bfloat16)
    return (query_grad, key_grad, value_grad)


def gather_kernel(slabs, stride, orders, widths, *refs):
    count = len(orders)
    sources, targets = refs[:count], refs[count : 2 * count]
    own_sems, send_sems, recv_sems = refs[2 * count :]
    bits = slabs.bit_length() - 1
    place, core = lax.axis_index("dp"), lax.axis_index("tp")
    me = place // stride
    index = [(me // (1 << b)) % 2 for b in range(bits)]

    def partner(b):
        here = index[b]
        return (place + (1 - 2 * here) * ((1 << b) * stride), core)

    sibling = (place, 1 - core)
    barrier = pltpu.get_barrier_semaphore()
    for b in range(bits):
        pl.semaphore_signal(barrier, inc=1, device_id=partner(b), device_id_type=MESH)
    pl.semaphore_signal(barrier, inc=1, device_id=sibling, device_id_type=MESH)
    pl.semaphore_wait(barrier, bits + 1)

    def view(target, done):
        where = tuple(slice(None) if b in done else index[b] for b in reversed(range(bits)))
        return target.at[(core,) + where]

    owns, copies = [], {}
    for i in range(count):
        source = sources[i]
        own = pltpu.make_async_copy(source, view(targets[i], ()), own_sems.at[i])
        own.start()
        owns.append(own)

    def start(i, step):
        if step == 0:
            source, target, device = sources[i], view(targets[i], ()), partner(orders[i][0])
        elif step < bits:
            source = target = view(targets[i], orders[i][:step])
            device = partner(orders[i][step])
        else:
            source = target = targets[i].at[core]
            device = sibling
        copy = pltpu.make_async_remote_copy(
            src_ref=source,
            dst_ref=target,
            send_sem=send_sems.at[i, step],
            recv_sem=recv_sems.at[i, step],
            device_id=device,
            device_id_type=MESH,
        )
        copy.start()
        copies[i, step] = copy

    ahead = 2
    for tick in range(count + (bits + 1) * ahead + 1):
        for step in range(bits + 1, -1, -1):
            i = tick - step * ahead
            if 0 <= i < count:
                if step > 0:
                    copies[i, step - 1].wait_recv()
                if step == 1:
                    owns[i].wait()
                if step <= bits:
                    start(i, step)
    for copy in copies.values():
        copy.wait_send()


def gather_weights(shards, orders, slabs, stride):
    bits = slabs.bit_length() - 1
    count = len(shards)
    shapes = [
        jax.ShapeDtypeStruct((2,) + (2,) * bits + s.shape, s.dtype) for s in shards
    ]
    full = pl.pallas_call(
        functools.partial(gather_kernel, slabs, stride, orders, None),
        out_shape=shapes,
        in_specs=[pl.BlockSpec(memory_space=pl.ANY)] * count,
        out_specs=[pl.BlockSpec(memory_space=pl.ANY)] * count,
        scratch_shapes=[
            pltpu.SemaphoreType.DMA((count,)),
            pltpu.SemaphoreType.DMA((count, bits + 1)),
            pltpu.SemaphoreType.DMA((count, bits + 1)),
        ],
        compiler_params=pltpu.CompilerParams(collective_id=0, has_side_effects=True),
        name="gather_weights",
    )(*shards)
    return [f.reshape((2, slabs * s.shape[0], s.shape[1])) for f, s in zip(full, shards)]


def beside(full):
    return jnp.concatenate([full[0], full[1]], axis=1)


def per_device(
    n_dp,
    tokens,
    segment_ids,
    cotangent,
    w_query,
    w_key,
    w_value,
    w_output,
    shared_down,
    shared_up,
    w_in,
    w_out,
    gain_one,
    gain_two,
    query_scale,
    query_bias,
    value_scale,
    value_bias,
):
    core = lax.axis_index("tp")
    rows = tokens.shape[0] // 2
    tokens = lax.dynamic_slice_in_dim(tokens, core * rows, rows, 0)
    cotangent = lax.dynamic_slice_in_dim(cotangent, core * rows, rows, 0)
    sequences = segment_ids.shape[0] // 2
    segment_ids = lax.dynamic_slice_in_dim(segment_ids, core * sequences, sequences, 0)

    down_half = shared_down.shape[1] // 2
    down_own = lax.dynamic_slice_in_dim(shared_down, core * down_half, down_half, 1)
    out_t = w_out.T
    quarter = w_in.shape[1] // 4
    shards = [w_query, w_key, w_value, w_output.T, down_own, shared_up]
    shards += [w_in[:, j * quarter : (j + 1) * quarter] for j in range(4)]
    shards += [out_t[:, j * quarter : (j + 1) * quarter] for j in range(4)]
    stride = 1
    while (w_query.shape[0] * stride) % TILE_ROWS or (shared_up.shape[0] * stride) % TILE_ROWS:
        stride *= 2
    if stride > 1:
        groups = [list(range(g * stride, (g + 1) * stride)) for g in range(n_dp // stride)]
        shards = [
            lax.all_gather(s, "dp", axis=0, tiled=True, axis_index_groups=groups) for s in shards
        ]
    slabs = n_dp // stride
    bits = slabs.bit_length() - 1
    far = list(range(bits - 1, -1, -1))
    first = tuple(far)
    second = tuple(far[:-2] + [0, 1])
    third = tuple([0, 1] + far[:-2])
    pick = {"A": first, "B": second, "C": third}
    orders = [pick[c] for c in "ABCABABCABABCA"]
    full = gather_weights(shards, orders, slabs, stride)
    query_full, key_full, value_full, output_t, down_full, up_full = [beside(f) for f in full[:6]]
    in_full = jnp.concatenate([full[6 + j][h] for h in range(2) for j in range(4)], axis=1)
    out_full_t = jnp.concatenate([full[10 + j][h] for h in range(2) for j in range(4)], axis=1)

    heads = query_full.shape[1] // HD
    projected = jnp.dot(tokens, down_full, preferred_element_type=jnp.float32)
    query_low = (projected * query_scale).astype(jnp.bfloat16)
    value_low = (projected * value_scale).astype(jnp.bfloat16)
    query_delta = jnp.dot(query_low, up_full, preferred_element_type=jnp.float32)
    value_delta = jnp.dot(value_low, up_full, preferred_element_type=jnp.float32)
    queries = (
        jnp.dot(tokens, query_full, preferred_element_type=jnp.float32) + query_bias * query_delta
    ).astype(jnp.bfloat16)
    keys = jnp.dot(tokens, key_full, preferred_element_type=jnp.float32).astype(jnp.bfloat16)
    values = (
        jnp.dot(tokens, value_full, preferred_element_type=jnp.float32) + value_bias * value_delta
    ).astype(jnp.bfloat16)
    split = (sequences, SEQ_LEN, heads, HD)
    query_blocks = queries.reshape(split)
    key_blocks = keys.reshape(split)
    value_blocks = values.reshape(split)
    mixed, logsum = lax.map(attend_forward, (query_blocks, key_blocks, value_blocks, segment_ids))
    mixed = mixed.reshape(rows, heads * HD)
    attention = times_transposed(mixed, output_t)
    normed_one, inverse_one = normalize(tokens.astype(jnp.float32) + attention)
    hidden = normed_one * gain_one
    hidden_low = hidden.astype(jnp.bfloat16)
    activation = jnp.dot(hidden_low, in_full, preferred_element_type=jnp.float32)
    inner, gelu_back = jax.vjp(exact_gelu, activation)
    branch = times_transposed(inner.astype(jnp.bfloat16), out_full_t)
    normed_two, inverse_two = normalize(hidden + branch)
    output = (normed_two * gain_two).astype(jnp.bfloat16)
    sum_two_grad = norm_back(cotangent.astype(jnp.float32), normed_two, inverse_two, gain_two)
    branch_grad = sum_two_grad.astype(jnp.bfloat16)
    inner_grad = jnp.dot(branch_grad, out_full_t, preferred_element_type=jnp.float32)
    (activation_grad,) = gelu_back(inner_grad)
    hidden_grad = sum_two_grad + times_transposed(activation_grad.astype(jnp.bfloat16), in_full)
    sum_one_grad = norm_back(hidden_grad, normed_one, inverse_one, gain_one)
    attention_grad = sum_one_grad.astype(jnp.bfloat16)
    mixed_grad = jnp.dot(attention_grad, output_t, preferred_element_type=jnp.float32).astype(
        jnp.bfloat16
    )
    query_grad, key_grad, value_grad = lax.map(
        attend_backward,
        (query_blocks, key_blocks, value_blocks, segment_ids, logsum, mixed_grad.reshape(split)),
    )
    query_grad = query_grad.reshape(rows, heads * HD)
    key_grad = key_grad.reshape(rows, heads * HD)
    value_grad = value_grad.reshape(rows, heads * HD)
    query_grad_wide = query_grad.astype(jnp.float32)
    value_grad_wide = value_grad.astype(jnp.float32)
    query_bias_part = jnp.sum(query_grad_wide * query_delta, axis=0)
    value_bias_part = jnp.sum(value_grad_wide * value_delta, axis=0)
    query_delta_grad = (query_grad_wide * query_bias).astype(jnp.bfloat16)
    value_delta_grad = (value_grad_wide * value_bias).astype(jnp.bfloat16)
    query_low_grad = times_transposed(query_delta_grad, up_full)
    value_low_grad = times_transposed(value_delta_grad, up_full)
    query_scale_part = jnp.sum(projected * query_low_grad, axis=0)
    value_scale_part = jnp.sum(projected * value_low_grad, axis=0)
    projected_grad = (query_low_grad * query_scale + value_low_grad * value_scale).astype(
        jnp.bfloat16
    )
    token_grad = (
        sum_one_grad
        + times_transposed(query_grad, query_full)
        + times_transposed(key_grad, key_full)
        + times_transposed(value_grad, value_full)
        + times_transposed(projected_grad, down_full)
    )
    sums = lax.psum(
        (query_scale_part, query_bias_part, value_scale_part, value_bias_part), ("dp", "tp")
    )
    return (output, token_grad) + sums


def solution(mesh):
    in_specs = (
        P("dp", None),
        P("dp", None),
        P("dp", None),
        P("dp", "tp"),
        P("dp", "tp"),
        P("dp", "tp"),
        P("tp", "dp"),
        P("dp", None),
        P("dp", "tp"),
        P("dp", "tp"),
        P("tp", "dp"),
        P(),
        P(),
        P(),
        P(),
        P(),
        P(),
    )
    out_specs = (P(("dp", "tp"), None), P(("dp", "tp"), None), P(), P(), P(), P())
    return jax.shard_map(
        functools.partial(per_device, mesh.shape["dp"]),
        mesh=mesh,
        in_specs=in_specs,
        out_specs=out_specs,
        check_vma=False,
    )
```

time: 787 us -> 418 us (0.53)
  blocking collectives: 253 us -> 39.2 us
  waiting for transfers between devices: 166 us -> 0 us
  Pallas kernels: 0 us -> 90.4 us
  matrix products: 208 us -> 159 us
  other arithmetic: 62.9 us -> 31.9 us
  local copies, waits for them, and re-layouts: 72.1 us -> 90.2 us
  between operations: 15.2 us -> 1.87 us
    all_gather x5 -> x0, blocking collectives: 212 us -> none  [the longest x1 47 us: per_device(): lax.all_gather(w_key, 'dp', axis=0, tiled=True)]
    pallas_call x0 -> x1, Pallas kernels: none -> 90.4 us  [gather_weights(): pl.pallas_call(functools.partial(gather_kernel, slabs, stride, orders, No...]
    all_gather x3 -> x0, waiting for transfers between devices: 89.5 us -> none  [the longest x1 59.8 us: per_device(): lax.all_gather(w_in, 'dp', axis=0, tiled=True)]
    psum x4 -> x0, waiting for transfers between devices: 73.5 us -> none  [the longest x1 26.8 us: per_device(): attention = lax.psum(attention_part, 'tp')]
    unnamed x94 -> x182, local copies, waits for them, and re-layouts: 16.7 us -> 34 us
    dot_general x2 -> x1, matrix products: 17.1 us -> 5.08 us  [per_device(): jnp.dot(attention_grad, output_t, preferred_element_type=jnp.float32)]
    mul x2 -> x0, other arithmetic: 9.52 us -> none  [norm_back(): return inverse * (scaled - first - normed * second)]
    reduce_sum x2 -> x0, other arithmetic: 8.69 us -> none  [normalize(): average = jnp.mean(values, axis=-1, keepdims=True)]
  transfers between devices with their start and end apart: 8 -> 0, of which waited for: 6 -> 0; matrix products, arithmetic and copies ran while one was open for 9% -> 0% of each run, Pallas kernels for 0% -> 0%
where the time goes in v1:
time: 418 us; the launch traced here: 413 us
  matrix products  159 us (38%)
  Pallas kernels  90.4 us (22%)
  local copies, waits for them, and re-layouts  90.2 us (22%)
  blocking collectives  39.2 us (9%)
  other arithmetic  31.9 us (8%)
    pallas_call x1, Pallas kernels, gather_weights(): pl.pallas_call(functools.partial(gather_kernel, slabs, stride, orders, No...  90.4 us
    dot_general x9, matrix products, times_transposed(): lax.dot_general(left, right, (((1,), (1,)), ((), ())), preferred_element_...  58.7 us
    psum x1, blocking collectives, per_device(): lax.psum((query_scale_part, query_bias_part, value_scale_part, value_bias...  39.2 us
    dot_general x1, matrix products, per_device(): jnp.dot(hidden_low, in_full, preferred_element_type=jnp.float32)  34 us
    unnamed x182, local copies, waits for them, and re-layouts  34 us
    convert_element_type x2, other arithmetic, attend_backward(): (probs * (prob_grad - jnp.sum(probs * prob_grad, axis=-1, keepdims=True))...  14.2 us
    dot_general x2, matrix products, attend_backward(): jnp.einsum('qhe,khe->hqk', mixed_grad, values, preferred_element_type=jnp...  13.8 us
    dot_general x2, matrix products, attend_forward(): jnp.einsum('hqk,khe->qhe', weights_low, values, preferred_element_type=jn...  11 us

profile of v1, /device:TPU:0, one launch (start us, length us, event | category | flops | bytes accessed | tf_op | source)
XLA Modules:
  0.0 412.9 jit_solution(12293545606956235152)
XLA Ops:
  5.1 90.4 %gather_weights.1 = (bf16[2,2,2,2,2,48,384]{6,5,4,3,2,1,0:T(8,128)(2,1)}, bf16[2,2,2,2,2,48,384]{6,5,4,3,2,1,0:T(8,128)(2,1)}, bf16[2,2,2,2,2,48,384]{6,5,4,3,2,...) custom-call(bf16[48,384]{1,0:T(8,128)(2,1)} %refs_0_.1, ...), custom_call_target="tpu_custom_call" | custom-call | tf_op jit(solution)/shard_map/gather_weights/pallas_call | solution.py:157
  97.1 3.8 constant_dynamic-slice_fusion.2
  100.9 1.8 fusion.91
  103.4 1.8 fusion.72
  114.1 4.2 %fusion.71 = f32[1024,768]{1,0:T(8,128)S(1)} fusion(f32[1024,1024]{1,0:T(8,128)} %copy-done.26, f32[1024]{0:T(1024)S(1)} %copy-done.70, bf16[1024,384]{1,0:T(8,128)(2,1)S(1)} %bitcast.194, bf16[1024,384]{1,0:T(8,128)(2,1)S(1)} %bitcast.190), kind=kOutput, calls=%fused_computation.115 | convolution fusion | flops 1615855616 | bytes 8916992 | tf_op jit(solution)/shard_map/dot_general | solution.py:237
  119.9 2.5 add_convert_fusion.4
  124.1 2.4 reshape.240
  126.5 3.0 copy.52
  131.8 2.5 convolution_convert_fusion.1
  136.1 2.4 reshape.242
  141.6 22.1 %while.26 = (s32[]{:T(128)}, bf16[2,512,12,64]{1,3,2,0:T(8,128)(2,1)}, f32[2,12,512]{2,1,0:T(8,128)}, bf16[2,512,12,64]{1,3,2,0:T(8,128)(2,1)}, s32[2,512]{1,0:T...) while((s32[]{:T(128)}, ...), condition=%wide.region_3.4_spmd, body=%wide.region_0.3_spmd.sunk | while | flops 843704320 | bytes 42156632 | solution.py:249
  142.0 2.1 fusion.164
  144.0 2.6 fusion.165
  147.2 5.5 %fusion.166 = bf16[2,512,12,64]{1,3,2,0:T(8,128)(2,1)} fusion(bf16[2,512,12,64]{1,3,2,0:T(8,128)(2,1)} %get-tuple-element.405, s32[]{:T(128)} %get-tuple-element.404, f32[12,512,512]{1,2,0:T(8,128)S(1)} %get-tuple-element.382, f32[12,512]{1,0:T(8,128)S(1)} %fusion.165, f32[12,512]{1,0:T(8,128)S(1)} %get-tuple-element.383, ...), kind=kOutput, calls=%fused_computation.8.clone.1 | convolution fusion | flops 418775040 | bytes 14468096 | tf_op jit(solution)/shard_map/while/body/eval_jaxpr/hqk,khe->qhe/dot_general | solution.py:57
  152.9 2.1 fusion.164
  155.0 2.6 fusion.165
  158.2 5.5 %fusion.166 = bf16[2,512,12,64]{1,3,2,0:T(8,128)(2,1)} fusion(bf16[2,512,12,64]{1,3,2,0:T(8,128)(2,1)} %get-tuple-element.405, s32[]{:T(128)} %get-tuple-element.404, f32[12,512,512]{1,2,0:T(8,128)S(1)} %get-tuple-element.382, f32[12,512]{1,0:T(8,128)S(1)} %fusion.165, f32[12,512]{1,0:T(8,128)S(1)} %get-tuple-element.383, ...), kind=kOutput, calls=%fused_computation.8.clone.1 | convolution fusion | flops 418775040 | bytes 14468096 | tf_op jit(solution)/shard_map/while/body/eval_jaxpr/hqk,khe->qhe/dot_general | solution.py:57
  163.7 4.2 %copy.55 = bf16[2,512,12,64]{1,0,3,2:T(2,128)(2,1)S(1)} copy(bf16[2,512,12,64]{1,3,2,0:T(8,128)(2,1)} %get-tuple-element.117) | data formatting | bytes 3145728 | tf_op jit(solution)/shard_map/while | solution.py:249
  169.5 2.6 copy.81
  172.1 3.6 fusion.129
  181.3 34.0 %fusion.57 = (f32[1024,3072]{1,0:T(8,128)}, f32[1024,3072]{1,0:T(8,128)}) fusion(bf16[768,3072]{1,0:T(8,128)(2,1)S(1)} %constant_dynamic-update-slice_fusion, f32[1024,768]{0,1:T(8,128)S(1)} %get-tuple-element.263, f32[768]{0:T(1024)S(1)} %copy-done.84, f32[1024]{0:T(1024)S(1)} %add_rsqrt_fusion.1, f32[1024]{0:T(1024)S(1)} %broadcast_multiply_fusion.5), kind=kOutput, calls=%fused_computation.65 | convolution fusion | flops 5030019072 | bytes 33041408 | tf_op jit(solution)/shard_map/dot_general | solution.py:255
  218.1 13.0 %fusion.130 = (f32[1024]{0:T(1024)S(1)}, f32[1024,768]{0,1:T(8,128)S(1)}) fusion(bf16[768,3072]{1,0:T(8,128)(2,1)S(1)} %constant_dynamic-update-slice_fusion.8, f32[1024,3072]{1,0:T(8,128)} %get-tuple-element.264, f32[1024,3072]{1,0:T(8,128)} %get-tuple-element.265, f32[768]{0:T(1024)S(1)} %copy-done.84, f32[1024]{0:T(1024)S(1)} %add_rsqrt_fusion.1, ...), kind=kOutput, calls=%fused_computation.204 | convolution fusion | flops 4845206528 | bytes 36191232 | tf_op jit(solution)/shard_map/dot_general | solution.py:33
  233.2 2.6 copy.82
  235.8 4.4 %fusion.70 = (f32[1024]{0:T(1024)S(1)}, f32[1024]{0:T(1024)S(1)}, bf16[1024,768]{0,1:T(8,128)(2,1)}) fusion(bf16[1024,768]{0,1:T(8,128)(2,1)} %copy.82, f32[768]{0:T(1024)S(1)} %copy-done.80, f32[1024]{0:T(1024)S(1)} %add_rsqrt_fusion, f32[1024,768]{0,1:T(8,128)} %copy-done.14, f32[1024]{0:T(1024)S(1)} %broadcast_multiply_fusion.4), kind=kLoop, calls=%fused_computation.104 | loop fusion | flops 7075840 | bytes 6310912 | tf_op jit(solution)/shard_map/reduce_sum | solution.py:27
  240.2 26.1 %fusion.112 = (f32[1024]{0:T(1024)S(1)}, f32[1024]{0:T(1024)S(1)}, f32[1024,768]{0,1:T(8,128)}) fusion(f32[1024]{0:T(1024)S(1)} %add_rsqrt_fusion.1, f32[1024,768]{0,1:T(8,128)S(1)} %get-tuple-element.263, f32[1024]{0:T(1024)S(1)} %broadcast_multiply_fusion.5, f32[768]{0:T(1024)S(1)} %copy-done.84, bf16[768,3072]{1,0:T(8,128)(2,1)} %copy-done.66, ...), kind=kOutput, calls=%fused_computation.186 | convolution fusion | flops 9726588928 | bytes 45651968 | tf_op jit(solution)/shard_map/dot_general | solution.py:33
  266.4 5.1 %convolution_convert_fusion = bf16[1024,768]{1,0:T(8,128)(2,1)} fusion(bf16[768,384]{1,0:T(8,128)(2,1)} %bitcast.230, bf16[768,384]{1,0:T(8,128)(2,1)} %bitcast.228, f32[1024,768]{0,1:T(8,128)} %get-tuple-element.268, f32[1024,768]{0,1:T(8,128)S(1)} %get-tuple-element.263, f32[1024]{0:T(1024)S(1)} %broadcast_multiply_fusion, ...), kind=kOutput, calls=%fused_computation.122 | convolution fusion | flops 1216610304 | bytes 9060352 | tf_op jit(solution)/shard_map/dot_general | solution.py:267
  279.9 50.5 %while.27 = (s32[]{:T(128)}, bf16[2,512,12,64]{1,3,2,0:T(8,128)(2,1)}, bf16[2,512,12,64]{1,3,2,0:T(8,128)(2,1)}, bf16[2,512,12,64]{1,3,2,0:T(8,128)(2,1)}, bf16[...) while((s32[]{:T(128)}, ...), condition=%wide.region_14.15_spmd, body=%wide.region_12.14_spmd.sunk | while | flops 2062673920 | bytes 147524944 | solution.py:270
  280.1 1.8 fusion.175
  283.0 6.9 %multiply_reduce_fusion.8 = (f32[12,512]{1,0:T(8,128)S(1)}, f32[12,512,512]{1,2,0:T(8,128)}) fusion(f32[12,512,512]{1,2,0:T(8,128)S(1)} %fusion.175, f32[12,512]{1,0:T(8,128)S(1)} %dynamic-slice_bitcast_fusion.2, pred[512,512]{0,1:T(8,128)(4,1)S(1)} %broadcast_compare_fusion.5, bf16[2,512,12,64]{1,3,2,0:T(8,128)(2,1)S(1)} %copy-done.9, ...), kind=kOutput, calls=%fused_computation.24.clone.1 | convolution fusion | flops 418375680 | bytes 27059200 | tf_op jit(solution)/shard_map/while/body/eval_jaxpr/qhe,khe->hqk/dot_general | solution.py:71
  289.8 7.1 %multiply_convert_fusion.15 = bf16[12,512,512]{1,2,0:T(8,128)(2,1)S(1)} fusion(f32[12,512,512]{1,2,0:T(8,128)} %get-tuple-element.394, f32[12,512,512]{1,2,0:T(8,128)S(1)} %fusion.175, f32[12,512]{1,0:T(8,128)S(1)} %get-tuple-element.395, f32[12,512]{1,0:T(8,128)S(1)} %dynamic-slice_bitcast_fusion.2, pred[512,512]{0,1:T(8,128)(4,1)S(1)} %broadcast_compare_fusion.5), kind=kLoop, calls=%fused_computation.23.clone.1 | loop fusion | flops 18874368 | bytes 31768576 | tf_op jit(solution)/shard_map/while/body/eval_jaxpr/convert_element_type | solution.py:72
  297.0 2.0 fusion.177
  301.3 3.9 fusion.178
  305.2 1.8 fusion.175
  308.1 6.9 %multiply_reduce_fusion.8 = (f32[12,512]{1,0:T(8,128)S(1)}, f32[12,512,512]{1,2,0:T(8,128)}) fusion(f32[12,512,512]{1,2,0:T(8,128)S(1)} %fusion.175, f32[12,512]{1,0:T(8,128)S(1)} %dynamic-slice_bitcast_fusion.2, pred[512,512]{0,1:T(8,128)(4,1)S(1)} %broadcast_compare_fusion.5, bf16[2,512,12,64]{1,3,2,0:T(8,128)(2,1)S(1)} %copy-done.9, ...), kind=kOutput, calls=%fused_computation.24.clone.1 | convolution fusion | flops 418375680 | bytes 27059200 | tf_op jit(solution)/shard_map/while/body/eval_jaxpr/qhe,khe->hqk/dot_general | solution.py:71
  315.0 7.1 %multiply_convert_fusion.15 = bf16[12,512,512]{1,2,0:T(8,128)(2,1)S(1)} fusion(f32[12,512,512]{1,2,0:T(8,128)} %get-tuple-element.394, f32[12,512,512]{1,2,0:T(8,128)S(1)} %fusion.175, f32[12,512]{1,0:T(8,128)S(1)} %get-tuple-element.395, f32[12,512]{1,0:T(8,128)S(1)} %dynamic-slice_bitcast_fusion.2, pred[512,512]{0,1:T(8,128)(4,1)S(1)} %broadcast_compare_fusion.5), kind=kLoop, calls=%fused_computation.23.clone.1 | loop fusion | flops 18874368 | bytes 31768576 | tf_op jit(solution)/shard_map/while/body/eval_jaxpr/convert_element_type | solution.py:72
  322.1 2.0 fusion.177
  326.4 3.9 fusion.178
  330.4 3.0 copy.66
  334.7 2.4 fusion.69
  340.3 2.6 copy.68
  343.0 2.9 fusion.67
  346.2 1.8 fusion.81
  348.4 3.9 multiply_reduce_fusion.1
  352.3 39.2 %all-reduce = (f32[1024]{0:T(1024)}, f32[768]{0:T(1024)}, f32[1024]{0:T(1024)}, f32[768]{0:T(1024)}) all-reduce(f32[1024]{0:T(1024)S(1)} %get-tuple-element.178, f32[768]{0:T(1024)S(1)} %fusion.67, f32[1024]{0:T(1024)S(1)} %get-tuple-element.177, f32[768]{0:T(1024)S(1)} %fusion.69), channel_id=1, replica_groups=mesh['dp'=16,'tp'=2] {'dp','tp'}, use_global_device_ids=true, to_apply=%region_16.17 | all-reduce | flops 3584 | bytes 28672 | tf_op jit(solution)/shard_map/psum | solution.py:297
  391.5 3.3 fusion.93
  400.6 1.8 fusion.73
  403.7 3.7 add_add_fusion
  407.4 3.7 copy.72
  (264 shorter events, 68.0 us)
Async XLA Ops:
  97.0 3.8 copy-start.28
  97.0 3.8 copy-start.30
  100.9 6.9 %copy-start.22 = (bf16[1024,768]{1,0:T(8,128)(2,1)}, bf16[1024,768]{1,0:T(8,128)(2,1)S(1)}, u32[]{:S(2)}) copy-start(bf16[1024,768]{1,0:T(8,128)(2,1)S(1)} %get-tuple-element.283) | copy-start | bytes 4718596
  103.4 3.1 copy-start.57
  105.3 3.5 copy-start.85
  114.1 5.8 %copy-start.23 = (bf16[1024,768]{1,0:T(8,128)(2,1)S(1)}, bf16[1024,768]{1,0:T(8,128)(2,1)}, u32[]{:S(2)}) copy-start(bf16[1024,768]{1,0:T(8,128)(2,1)} %copy-done.22) | copy-start | bytes 4718596
  114.1 5.8 %copy-start.41 = (bf16[1,2,2,2,2,48,384]{6,5,4,3,2,1,0:T(8,128)(2,1)S(1)}, bf16[1,2,2,2,2,48,384]{6,5,4,3,2,1,0:T(8,128)(2,1)}, u32[]{:S(2)}) copy-start(bf16[1,2,2,2,2,48,384]{6,5,4,3,2,1,0:T(8,128)(2,1)} %get-tuple-element.280) | copy-start | bytes 1769476
  114.1 5.8 %copy-start.43 = (bf16[1,2,2,2,2,48,384]{6,5,4,3,2,1,0:T(8,128)(2,1)S(1)}, bf16[1,2,2,2,2,48,384]{6,5,4,3,2,1,0:T(8,128)(2,1)}, u32[]{:S(2)}) copy-start(bf16[1,2,2,2,2,48,384]{6,5,4,3,2,1,0:T(8,128)(2,1)} %get-tuple-element.281) | copy-start | bytes 1769476
  114.1 5.8 %copy-start.81 = (f32[768]{0:T(1024)S(1)}, f32[768]{0:T(1024)}, u32[]{:S(2)}) copy-start(f32[768]{0:T(1024)} %param.37) | copy-start | bytes 9220
  126.5 3.0 copy-start.54
  126.5 3.0 copy-start.55
  136.1 4.1 copy-start.83
  163.7 5.8 %copy-start.2 = (bf16[2,512,12,64]{1,3,2,0:T(8,128)(2,1)}, bf16[2,512,12,64]{1,3,2,0:T(8,128)(2,1)S(1)}, u32[]{:S(2)}) copy-start(bf16[2,512,12,64]{1,3,2,0:T(8,128)(2,1)S(1)} %get-tuple-element.453) | copy-start | bytes 4718596
  163.7 5.8 %copy-start.4 = (bf16[2,512,12,64]{1,3,2,0:T(8,128)(2,1)}, bf16[2,512,12,64]{1,3,2,0:T(8,128)(2,1)S(1)}, u32[]{:S(2)}) copy-start(bf16[2,512,12,64]{1,3,2,0:T(8,128)(2,1)S(1)} %get-tuple-element.454) | copy-start | bytes 4718596
  163.7 5.8 %copy-start.64 = (s32[2,512]{1,0:T(2,128)}, s32[2,512]{1,0:T(2,128)S(1)}, u32[]{:S(2)}) copy-start(s32[2,512]{1,0:T(2,128)S(1)} %get-tuple-element.456) | copy-start | bytes 12292
  175.7 90.7 %copy-start.12 = (f32[1024,768]{0,1:T(8,128)}, f32[1024,768]{0,1:T(8,128)S(1)}, u32[]{:S(2)}) copy-start(f32[1024,768]{0,1:T(8,128)S(1)} %get-tuple-element.263) | copy-start | bytes 9437188
  175.8 90.6 %copy-start.68 = (f32[1024]{0:T(1024)}, f32[1024]{0:T(1024)S(1)}, u32[]{:S(2)}) copy-start(f32[1024]{0:T(1024)S(1)} %broadcast_multiply_fusion.5) | copy-start | bytes 12292
  176.2 90.2 %copy-start.74 = (f32[1024]{0:T(1024)}, f32[1024]{0:T(1024)S(1)}, u32[]{:S(2)}) copy-start(f32[1024]{0:T(1024)S(1)} %add_rsqrt_fusion.1) | copy-start | bytes 12292
  181.3 34.1 %copy-start.66 = (bf16[768,3072]{1,0:T(8,128)(2,1)}, bf16[768,3072]{1,0:T(8,128)(2,1)S(1)}, u32[]{:S(2)}) copy-start(bf16[768,3072]{1,0:T(8,128)(2,1)S(1)} %constant_dynamic-update-slice_fusion) | copy-start | bytes 14155780
  181.3 34.1 %copy-start.48 = (bf16[2,2,2,2,2,48,384]{6,5,4,3,2,1,0:T(8,128)(2,1)S(1)}, bf16[2,2,2,2,2,48,384]{6,5,4,3,2,1,0:T(8,128)(2,1)}, u32[]{:S(2)}) copy-start(bf16[2,2,2,2,2,48,384]{6,5,4,3,2,1,0:T(8,128)(2,1)} %get-tuple-element.123) | copy-start | bytes 3538948
  181.3 34.0 %copy-start.49 = (bf16[2,2,2,2,2,48,384]{6,5,4,3,2,1,0:T(8,128)(2,1)S(1)}, bf16[2,2,2,2,2,48,384]{6,5,4,3,2,1,0:T(8,128)(2,1)}, u32[]{:S(2)}) copy-start(bf16[2,2,2,2,2,48,384]{6,5,4,3,2,1,0:T(8,128)(2,1)} %get-tuple-element.124) | copy-start | bytes 3538948
  218.1 13.0 %copy-start.67 = (bf16[768,3072]{1,0:T(8,128)(2,1)}, bf16[768,3072]{1,0:T(8,128)(2,1)S(1)}, u32[]{:S(2)}) copy-start(bf16[768,3072]{1,0:T(8,128)(2,1)S(1)} %constant_dynamic-update-slice_fusion.8) | copy-start | bytes 14155780
  232.8 3.0 copy-start.80
  266.4 5.1 %copy-start.76 = (f32[1024]{0:T(1024)}, f32[1024]{0:T(1024)S(1)}, u32[]{:S(2)}) copy-start(f32[1024]{0:T(1024)S(1)} %broadcast_multiply_fusion) | copy-start | bytes 12292
  266.4 5.1 %copy-start.78 = (f32[1024]{0:T(1024)}, f32[1024]{0:T(1024)S(1)}, u32[]{:S(2)}) copy-start(f32[1024]{0:T(1024)S(1)} %broadcast_multiply_fusion.1) | copy-start | bytes 12292
  275.9 4.0 copy-start.3
  275.9 4.0 copy-start.5
  275.9 4.0 copy-start.65
  289.8 7.1 %copy-start.18 = (bf16[2,512,12,64]{1,3,2,0:T(8,128)(2,1)S(1)}, bf16[2,512,12,64]{1,3,2,0:T(8,128)(2,1)}, u32[]{:S(2)}) copy-start(bf16[2,512,12,64]{1,3,2,0:T(8,128)(2,1)} %get-tuple-element.433) | copy-start | bytes 4718596 | tf_op jit(solution)/shard_map/while
  315.0 7.1 %copy-start.18 = (bf16[2,512,12,64]{1,3,2,0:T(8,128)(2,1)S(1)}, bf16[2,512,12,64]{1,3,2,0:T(8,128)(2,1)}, u32[]{:S(2)}) copy-start(bf16[2,512,12,64]{1,3,2,0:T(8,128)(2,1)} %get-tuple-element.433) | copy-start | bytes 4718596 | tf_op jit(solution)/shard_map/while
  342.9 2.9 copy-start.25
  342.9 3.0 copy-start.34
  342.9 3.3 copy-start.37
  342.9 3.3 copy-start.86
  348.4 3.9 copy-start.6
  391.5 3.3 copy-start.20
  396.9 3.5 copy-start.8
  396.9 3.6 copy-start.29
  396.9 3.6 copy-start.71
  396.9 3.6 copy-start.73
  400.5 2.9 copy-start.42
  400.6 3.1 copy-start.44
  400.6 3.1 copy-start.69
  400.6 3.1 copy-start.75
  400.6 3.1 copy-start.77
  400.6 3.1 copy-start.79
  407.4 3.7 copy-start.21
  407.4 5.2 %copy-start.1 = (bf16[48,1024]{1,0:T(8,128)(2,1)S(1)}, bf16[48,1024]{1,0:T(8,128)(2,1)}, u32[]{:S(2)}) copy-start(bf16[48,1024]{1,0:T(8,128)(2,1)} %param.28) | copy-start | bytes 294916
  (46 other events, 84.7 us)

commit v2 on v1

v2 whole, which is shorter than its diff:
```python
import functools
import math
import types

import jax
import jax.numpy as jnp
from jax import lax
from jax.experimental import pallas as pl
from jax.experimental.pallas import tpu as pltpu
from jax.sharding import PartitionSpec as P

HD = 64
SEQ_LEN = 512
SPAN = SEQ_LEN // 2
LABELS = 8
LANES = 128
SLABS = 16
COPIES = 4
MASKED = -1000000000.0
MESH = pl.DeviceIdType.MESH
VMEM_LIMIT = 62 << 20


def dot(left, right):
    return jnp.dot(left, right, preferred_element_type=jnp.float32)


def dot_nt(left, right):
    return lax.dot_general(
        left, right, (((1,), (1,)), ((), ())), preferred_element_type=jnp.float32
    )


def dot_tn(left, right):
    return lax.dot_general(
        left, right, (((0,), (0,)), ((), ())), preferred_element_type=jnp.float32
    )


def normalize(values):
    average = jnp.mean(values, axis=-1, keepdims=True)
    centered = values - average
    variance = jnp.mean(centered * centered, axis=-1, keepdims=True)
    inverse = lax.rsqrt(variance + 1e-05)
    return centered * inverse, inverse


def norm_back(scaled, normed, inverse):
    first = jnp.mean(scaled, axis=-1, keepdims=True)
    second = jnp.mean(scaled * normed, axis=-1, keepdims=True)
    return inverse * (scaled - first - normed * second)


def gelu_and_slope(values):
    below = 0.5 * lax.erf(values * (1.0 / math.sqrt(2.0))) + 0.5
    bell = jnp.exp(values * values * -0.5) * (1.0 / math.sqrt(2.0 * math.pi))
    return values * below, below + values * bell


def own_lanes(pair):
    lane = lax.broadcasted_iota(jnp.int32, pair.shape, 1)
    zeros = jnp.zeros_like(pair)
    return jnp.concatenate([jnp.where(lane < HD, pair, zeros), jnp.where(lane < HD, zeros, pair)])


def join_heads(wide):
    n = wide.shape[1] // 2
    return jnp.concatenate([wide[:HD, :n], wide[HD:, n:]]).T


def label_rows(row):
    kind = lax.broadcasted_iota(jnp.int32, (LABELS, SEQ_LEN), 0)
    hot = jnp.where(kind == row, 1.0, 0.0)
    many = jnp.sum(hot, axis=1, keepdims=True)
    which = lax.broadcasted_iota(jnp.int32, (LABELS, 1), 0)
    first = jnp.min(jnp.where(many == float(SPAN), which, LABELS), axis=0, keepdims=True)
    start = jnp.sum(jnp.where(row < first, 1, 0), axis=1, keepdims=True)
    return hot, start


def roll_matrix(start, back):
    here = lax.broadcasted_iota(jnp.int32, (SEQ_LEN, SEQ_LEN), 1 if back else 0)
    there = lax.broadcasted_iota(jnp.int32, (SEQ_LEN, SEQ_LEN), 0 if back else 1)
    moved = here + start
    moved = jnp.where(moved >= SEQ_LEN, moved - SEQ_LEN, moved)
    return jnp.where(moved == there, 1.0, 0.0).astype(jnp.bfloat16)


PIECES = ((0, 0), (0, 1), (0, 3), (1, 0), (1, 0), (1, 1), (4, 1), (6, 0), (2, 0), (2, 2), (2, 1), (3, 0), (3, 0), (3, 2), (7, 1), (8, 2), (9, 0), (10, 1), (11, 0), (12, 1), (13, 3), (5, 1))
PLAN = (
    (0, (48, 24, 32, 8)),
    (1, (25, 40, 9, 0, 16, 41, 17, 112, 33, 1, 10, 56, 120, 49, 42, 26, 27, 34, 18, 57, 2, 11, 50, 19, 58, 3, 152, 153, 136, 35, 43, 113, 4, 121, 20, 51, 128, 59, 12)),
    (2, (64, 72, 73, 96, 80, 65, 88, 104, 97, 105, 89, 81, 66, 74, 160, 28, 114, 98, 129, 82, 90, 106, 144, 60, 75, 67, 83, 44, 91, 107, 99, 122, 130, 29, 36, 37, 45)),
    (3, (76, 68, 84, 115, 145, 154, 92, 161, 100, 137, 168, 52, 108, 69, 77, 85)),
    (4, (131, 93, 101, 109)),
    (0, {1: (146, 123), 2: (155,), 3: (162, 138)}),
    (-1, (116, 53)),
    (1, {1: (147,)}),
    (-1, (169, 139, 61)),
    (2, {1: (124,), 2: (156, 163, 132, 117), 4: (125,), 5: (148,), 6: (140, 170, 133)}),
    (-1, (141, 149, 157)),
    (3, {1: (164,)}),
    (5, ()),
    (-1, (171, 165)),
    (4, {}),
    (-1, (5, 13, 21)),
    (5, {2: (172,)}),
    (-1, (173,)),
    (6, {}),
)


def layer_kernel(stride, bits, groups, names, *refs):
    r = types.SimpleNamespace(**dict(zip(names, refs)))
    buffers = refs[len(names) :]
    place, core = lax.axis_index("dp"), lax.axis_index("tp")
    me = place // stride
    index = [(me // (1 << b)) % 2 for b in range(bits)]
    width = r.w_query.shape[1]
    rows, model = r.tok.shape
    quarters = r.win.shape[-1] // model
    seqs = rows // SEQ_LEN
    pairs = 2 * width // LANES
    bf16 = jnp.bfloat16

    def partner(b):
        return (place + (1 - 2 * index[b]) * ((1 << b) * stride), core)

    sibling = (place, 1 - core)

    far = list(range(bits - 1, -1, -1))
    near = far[:-2]
    orders = (tuple(far), tuple(near + [0, 1]), tuple([0, 1] + near), tuple([1, 0] + near))
    ranks = r.down.shape[1]
    half_rank = ranks // 2
    shards = [
        (r.up, r.up_full, width, 0),
        (r.w_key, r.key_full, width, 0),
        (r.query_own, r.query_full, width, 0),
        (r.value_own, r.value_full, width, 0),
        (r.out_t, r.out_full, width, 0),
        (r.down, r.down_full, half_rank, core * half_rank),
    ]
    shards += [(r.w_in, r.win, width, j * width) for j in range(quarters)]
    shards += [(r.ff_t, r.wout, width, j * width) for j in range(quarters)]
    seen, pieces = {}, []
    for name, order in PIECES:
        seen[name] = seen.get(name, 0) + 1
    taken = {}
    for name, order in PIECES:
        source, target, columns, offset = shards[name]
        part = columns // seen[name]
        at = taken.get(name, 0)
        taken[name] = at + 1
        first = offset + at * part
        if not isinstance(first, int):
            first = pl.multiple_of(first, LANES)
        wide = offset * 2 if isinstance(offset, int) else 0
        spot = pl.ds(pl.multiple_of(core * columns + wide + at * part, LANES), part)
        pieces.append((source.at[:, pl.ds(first, part)], target, spot, orders[order]))

    def view(i, done):
        where = tuple(slice(None) if b in done else index[b] for b in reversed(range(bits)))
        return pieces[i][1].at[where + (slice(None), pieces[i][2])]

    def own(i):
        return pltpu.make_async_copy(pieces[i][0], view(i, ()), r.own_sems.at[i])

    def remote(i, step):
        source, _, _, order = pieces[i]
        there = view(i, order[:step])
        return pltpu.make_async_remote_copy(
            src_ref=source if step == 0 else there,
            dst_ref=there,
            send_sem=r.send_sems.at[i, step],
            recv_sem=r.recv_sems.at[i, step],
            device_id=partner(order[step]) if step < bits else sibling,
            device_id_type=MESH,
        )

    def move(i, step):
        if step > 0:
            remote(i, step - 1).wait_recv()
        if step == 0:
            own(i).start()
        if step == 1:
            own(i).wait()
        if step <= bits:
            remote(i, step).start()

    def fetch(n, source, target):
        return pltpu.make_async_copy(source, target, r.in_sems.at[n])

    mine = pl.ds(pl.multiple_of(core * rows, rows), rows)
    get_tokens = fetch(0, r.tokens.at[mine], r.raw)
    get_cotangent = fetch(1, r.cotangent.at[mine], r.raw)

    def seq_rows(s):
        return pl.ds(pl.multiple_of(s * SEQ_LEN, SEQ_LEN), SEQ_LEN)

    def full(ref, first=0, count=None):
        value = ref[..., pl.ds(first, count or ref.shape[-1])]
        return value.reshape((value.shape[-2] * (1 << bits), value.shape[-1]))

    def prep():
        get_tokens.wait()
        every = r.segments[...]
        held = jnp.where(core == 0, every[:seqs], every[seqs:])
        found = []
        for s in range(seqs):
            hot, start = label_rows(held[s : s + 1])
            turn = roll_matrix(start, False)
            r.turn[s] = turn
            part = pl.ds(s * SEQ_LEN, SEQ_LEN)
            r.tok[part, :] = dot(turn, r.raw[part, :]).astype(bf16)
            turned = dot_nt(hot.astype(bf16), turn)[:, SPAN:]
            r.same[s] = dot_tn(turned, turned)
            found.append(jnp.where(start < SEQ_LEN, 0.0, MASKED))
        lowest = functools.reduce(jnp.minimum, found)
        r.lowest[...] = jnp.broadcast_to(lowest, r.lowest.shape)
        get_cotangent.start()

    def merge():
        columns = pl.ds(pl.multiple_of(core * width, width), width)
        up_half = r.up_full[..., columns]
        up_half = up_half.reshape((up_half.shape[-2] * (1 << bits), width))
        down = r.down[...].astype(jnp.float32)
        for scale, bias, weight, target in (
            (r.query_scale, r.query_bias, r.w_query, r.query_own),
            (r.value_scale, r.value_bias, r.w_value, r.value_own),
        ):
            scaled = (down * scale[...][None, :]).astype(bf16)
            extra = dot(scaled, up_half) * bias[columns][None, :]
            target[...] = (weight[...].astype(jnp.float32) + extra).astype(bf16)

    def project(weight, target, factor):
        def body(s, _):
            value = dot(r.tok[seq_rows(s), :], full(weight))
            target[seq_rows(s), :] = (value * factor).astype(bf16)
            return 0

        lax.fori_loop(0, seqs, body, 0)

    quads = [(s, half) for s in range(seqs) for half in range(2)]

    def masked(scores, s, half):
        if half == 0:
            return scores
        same = r.same[s] > 0.5
        return jnp.where(jnp.concatenate([same, same], axis=1), scores, MASKED)

    def attend(p):
        columns = pl.ds(pl.multiple_of(p * LANES, LANES), LANES)
        places = [pl.ds(s * SEQ_LEN + half * SPAN, SPAN) for s, half in quads]
        scores = [
            dot_nt(r.keys[here, columns], own_lanes(r.queries[here, columns])) for here in places
        ]
        powers, totals = [], []
        for n, (s, half) in enumerate(quads):
            score = masked(scores[n], s, half)
            top = jnp.max(score, axis=0, keepdims=True)
            power = jnp.exp(score - top)
            total = jnp.sum(power, axis=0, keepdims=True)
            r.logsum[n, pl.ds(p, 1), :] = top + jnp.log(total)
            r.lowest[n : n + 1, :] = jnp.minimum(r.lowest[n : n + 1, :], top)
            powers.append(power.astype(bf16))
            totals.append(total)
        for n, here in enumerate(places):
            mixed = dot(r.values[here, columns].T, powers[n]) * (1.0 / totals[n])
            r.mixed[here, columns] = join_heads(mixed).astype(bf16)

    def attend_back(p):
        columns = pl.ds(pl.multiple_of(p * LANES, LANES), LANES)
        places = [pl.ds(s * SEQ_LEN + half * SPAN, SPAN) for s, half in quads]
        queries = [own_lanes(r.queries[here, columns]) for here in places]
        grads = [own_lanes(r.mixed[here, columns]) for here in places]
        scores = [dot_nt(r.keys[here, columns], queries[n]) for n, here in enumerate(places)]
        firsts = [dot_nt(r.values[here, columns], grads[n]) for n, here in enumerate(places)]
        probs, lows = [], []
        for n, (s, half) in enumerate(quads):
            prob = jnp.exp(masked(scores[n], s, half) - r.logsum[n, pl.ds(p, 1), :])
            both = prob * firsts[n]
            total = jnp.sum(both, axis=0, keepdims=True)
            probs.append(prob.astype(bf16))
            lows.append((both - prob * total).astype(bf16))
        for n, here in enumerate(places):
            value_grad = dot(probs[n], grads[n])
            key_grad = dot(lows[n], queries[n])
            query_grad = join_heads(dot(r.keys[here, columns].T, lows[n]))
            for a, grad in enumerate((query_grad * (1.0 / math.sqrt(HD)), key_grad, value_grad)):
                spot = pl.ds(pl.multiple_of(a * model + p * LANES, LANES), LANES)
                r.inner[here, spot] = grad.astype(bf16)

    def first_norm(s):
        here = seq_rows(s)
        attention = dot_nt(r.mixed[here, :], full(r.out_full))
        normed, inverse = normalize(r.tok[here, :].astype(jnp.float32) + attention)
        r.normed[here, :] = normed
        r.inverse[here, :] = jnp.broadcast_to(inverse, (SEQ_LEN, LANES))
        r.hidden[here, :] = (normed * r.gain_one[...][None, :]).astype(bf16)

    def widen(it):
        j, s = it // seqs, it % seqs
        columns = pl.ds(pl.multiple_of(j * model, model), model)
        weight = r.win[..., columns]
        weight = weight.reshape((model, model))
        for n in range(SEQ_LEN // LANES):
            here = pl.ds(pl.multiple_of(s * SEQ_LEN + n * LANES, LANES), LANES)
            inner, slope = gelu_and_slope(dot(r.hidden[here, :], weight))
            r.inner[here, columns] = inner.astype(bf16)
            r.slope[here, columns] = slope.astype(bf16)

    most = (quarters - 1) * model

    def narrow(s):
        here = seq_rows(s)
        r.wide[here, :] = dot_nt(r.inner[here, :most], full(r.wout, 0, most))

    def second_norm(s):
        here = seq_rows(s)
        normed_one = r.normed[here, :]
        gain_one, gain_two = r.gain_one[...][None, :], r.gain_two[...][None, :]
        branch = r.wide[here, :] + dot_nt(r.inner[here, most:], full(r.wout, most, model))
        normed, inverse = normalize(normed_one * gain_one + branch)
        r.hidden[here, :] = (normed * gain_two).astype(bf16)
        turned = dot(r.turn[s], r.raw[here, :])
        grad = norm_back(turned * gain_two, normed, inverse)
        low = grad.astype(bf16)
        for j in range(quarters):
            inner_grad = dot(low, full(r.wout, j * model, model))
            slope = r.slope[here, pl.ds(j * model, model)].astype(jnp.float32)
            low_grad = (inner_grad * slope).astype(bf16)
            grad = grad + dot_nt(low_grad, full(r.win, j * model, model))
        back = norm_back(grad * gain_one, normed_one, r.inverse[here, :][:, :1])
        r.wide[here, :] = back
        r.mixed[here, :] = dot(back.astype(bf16), full(r.out_full)).astype(bf16)

    def rank(n):
        block = 2 * LANES
        columns = pl.ds(pl.multiple_of(n * block, block), block)
        eye = jnp.where(
            lax.broadcasted_iota(jnp.int32, (block, block), 0)
            == lax.broadcasted_iota(jnp.int32, (block, block), 1),
            1.0,
            0.0,
        ).astype(bf16)
        down = r.down_full[..., columns]
        down = down.reshape((down.shape[-2] * (1 << bits), block))
        down_t = dot_nt(eye, down).astype(bf16)
        r.projected[columns, :] = dot_nt(down_t, r.tok[...]).astype(bf16)

    def adapters(n):
        part = pl.ds(pl.multiple_of(n * 2 * LANES, 2 * LANES), 2 * LANES)
        low = r.projected[part, :]
        up = r.up_full[n // 2, n % 2].reshape((2 * LANES, model)).astype(jnp.float32)
        for a, first, scales, bias in (
            (0, 0, r.query_scale, r.query_bias),
            (2, 2 * model, r.value_scale, r.value_bias),
        ):
            product = dot(low, r.inner[:, first : first + model]) * up
            scale = jnp.broadcast_to(scales[part][None, :], (LANES, 2 * LANES)).T
            r.sums[a + 1 : a + 2, :model] += jnp.sum(product * scale[:, :1], axis=0, keepdims=True)
            over = jnp.sum(product * bias[...][None, :], axis=1, keepdims=True)
            r.sums[a : a + 1, part] = jnp.broadcast_to(over, (2 * LANES, LANES)).T[:1]

    def finish(s):
        here = seq_rows(s)
        grad = r.wide[here, :]
        for a, weight in enumerate((r.query_full, r.key_full, r.value_full)):
            grad = grad + dot_nt(r.inner[here, a * model : (a + 1) * model], full(weight))
        r.wide[here, :] = dot_tn(r.turn[s], grad.astype(bf16))

    def give(n, s, source, target):
        part = pl.ds(s * SEQ_LEN, SEQ_LEN)
        return pltpu.make_async_copy(source.at[part], target.at[part], r.out_sems.at[n, s])

    def peer(group, flip):
        there, other = place, core
        for n, bit in enumerate(group):
            if flip & (1 << n):
                if bit < 0:
                    other = 1 - core
                else:
                    there = there + (1 - 2 * ((place // (1 << bit)) % 2)) * (1 << bit)
        return (there, other)

    def spread(g):
        group, buffer = groups[g], buffers[g]
        digits = [core if bit < 0 else (place // (1 << bit)) % 2 for bit in group]
        mine = sum(digit * (1 << n) for n, digit in enumerate(digits))
        before = sum((1 << len(one)) - 1 for one in groups[:g])
        return [
            pltpu.make_async_remote_copy(
                src_ref=buffer.at[mine],
                dst_ref=buffer.at[mine],
                send_sem=r.total_sends.at[before + flip - 1],
                recv_sem=r.total_recvs.at[before + flip - 1],
                device_id=peer(group, flip),
                device_id_type=MESH,
            )
            for flip in range(1, 1 << len(group))
        ], mine

    def send_sums(g, value):
        copies, mine = spread(g)
        buffers[g][mine] = value
        for copy in copies:
            copy.start()

    def take_sums(g):
        for copy in spread(g)[0]:
            copy.wait_recv()
        value = buffers[g][0]
        for n in range(1, 1 << len(groups[g])):
            value = value + buffers[g][n]
        return value

    get_tokens.start()
    barrier = pltpu.get_barrier_semaphore()
    near_by = [partner(b) for b in range(bits)] + [sibling]
    near_by += [peer(g, flip) for g in groups for flip in range(1, 1 << len(g))]
    for device in near_by:
        pl.semaphore_signal(barrier, inc=1, device_id=device, device_id_type=MESH)
    pl.semaphore_wait(barrier, len(near_by))

    loops = (
        (pairs, attend),
        (seqs, first_norm),
        (quarters * seqs, widen),
        (seqs, narrow),
        (seqs, second_norm),
        (pairs, attend_back),
        (ranks // (2 * LANES), rank),
    )
    blocks = (
        prep,
        merge,
        lambda: project(r.key_full, r.keys, 1.0),
        lambda: project(r.query_full, r.queries, 1.0 / math.sqrt(HD)),
        lambda: project(r.value_full, r.values, 1.0),
        get_cotangent.wait,
    )

    def run_loop(count, body, inside):
        def step(it, _):
            for when, some in inside.items():

                @pl.when(it == when)
                def _(some=some):
                    for one in some:
                        move(one // 8, one % 8)

            body(it)
            return 0

        lax.fori_loop(0, count, step, 0)

    for block, moves in PLAN:
        if isinstance(moves, tuple):
            for one in moves:
                move(one // 8, one % 8)
            if block >= 0:
                blocks[block]()
        else:
            run_loop(*loops[block], moves)

    for s in range(seqs):
        here = seq_rows(s)
        r.raw[here, :] = dot_tn(r.turn[s], r.hidden[here, :]).astype(bf16)
        give(0, s, r.raw, r.o_output).start()
    r.sums[...] = jnp.zeros_like(r.sums)
    run_loop(ranks // (2 * LANES), adapters, {})
    lowest = jnp.min(jnp.min(r.lowest[...], axis=1, keepdims=True), axis=0, keepdims=True)
    r.sums[1:2, model : model + LANES] = jnp.broadcast_to(
        jnp.where(lowest > 0.5 * MASKED, 0.0, 1.0), (1, LANES)
    )
    for g in range(len(groups)):
        send_sums(g, r.sums[...] if g == 0 else total)
        if g < seqs:
            finish(g)
            give(1, g, r.wide, r.o_grad).start()
        total = take_sums(g)
    r.o_sums[...] = total
    r.o_flag[...] = total[1:2, model : model + 1]
    for i in range(len(pieces)):
        for step in range(bits + 1):
            remote(i, step).wait_send()
    for g in range(len(groups)):
        for copy in spread(g)[0]:
            copy.wait_send()
    for s in range(seqs):
        give(0, s, r.raw, r.o_output).wait()
        give(1, s, r.wide, r.o_grad).wait()


def hand_kernel(grad, output, sums, o_grad, o_output, *refs):
    held, sems = refs[4:6], refs[6]
    gets, puts = [], []
    for n, (source, middle, target) in enumerate(
        ((grad, held[0], o_grad), (output, held[1], o_output))
    ):
        rows = source.shape[0] // COPIES
        for c in range(COPIES):
            part = pl.ds(c * rows, rows)
            gets.append(pltpu.make_async_copy(source.at[part], middle.at[part], sems.at[0, n, c]))
            puts.append(pltpu.make_async_copy(middle.at[part], target.at[part], sems.at[1, n, c]))
    for get in gets:
        get.start()
    for n, out in enumerate(refs[:4]):
        out[...] = sums[n, : out.shape[0]]
    for get, put in zip(gets, puts):
        get.wait()
        put.start()
    for put in puts:
        put.wait()


def gather_kernel(slabs, stride, orders, *refs):
    count = len(orders)
    sources, targets = refs[:count], refs[count : 2 * count]
    own_sems, send_sems, recv_sems = refs[2 * count :]
    bits = slabs.bit_length() - 1
    place, core = lax.axis_index("dp"), lax.axis_index("tp")
    me = place // stride
    index = [(me // (1 << b)) % 2 for b in range(bits)]

    def partner(b):
        here = index[b]
        return (place + (1 - 2 * here) * ((1 << b) * stride), core)

    sibling = (place, 1 - core)
    barrier = pltpu.get_barrier_semaphore()
    for b in range(bits):
        pl.semaphore_signal(barrier, inc=1, device_id=partner(b), device_id_type=MESH)
    pl.semaphore_signal(barrier, inc=1, device_id=sibling, device_id_type=MESH)
    pl.semaphore_wait(barrier, bits + 1)

    def view(target, done):
        where = tuple(slice(None) if b in done else index[b] for b in reversed(range(bits)))
        return target.at[(core,) + where]

    owns, copies = [], {}
    for i in range(count):
        source = sources[i]
        own = pltpu.make_async_copy(source, view(targets[i], ()), own_sems.at[i])
        own.start()
        owns.append(own)

    def start(i, step):
        if step == 0:
            source, target, device = sources[i], view(targets[i], ()), partner(orders[i][0])
        elif step < bits:
            source = target = view(targets[i], orders[i][:step])
            device = partner(orders[i][step])
        else:
            source = target = targets[i].at[core]
            device = sibling
        copy = pltpu.make_async_remote_copy(
            src_ref=source,
            dst_ref=target,
            send_sem=send_sems.at[i, step],
            recv_sem=recv_sems.at[i, step],
            device_id=device,
            device_id_type=MESH,
        )
        copy.start()
        copies[i, step] = copy

    ahead = 2
    for tick in range(count + (bits + 1) * ahead + 1):
        for step in range(bits + 1, -1, -1):
            i = tick - step * ahead
            if 0 <= i < count:
                if step > 0:
                    copies[i, step - 1].wait_recv()
                if step == 1:
                    owns[i].wait()
                if step <= bits:
                    start(i, step)
    for copy in copies.values():
        copy.wait_send()


def gather_weights(shards, orders, slabs, stride):
    bits = slabs.bit_length() - 1
    count = len(shards)
    shapes = [
        jax.ShapeDtypeStruct((2,) + (2,) * bits + s.shape, s.dtype) for s in shards
    ]
    full = pl.pallas_call(
        functools.partial(gather_kernel, slabs, stride, orders),
        out_shape=shapes,
        in_specs=[pl.BlockSpec(memory_space=pl.ANY)] * count,
        out_specs=[pl.BlockSpec(memory_space=pl.ANY)] * count,
        scratch_shapes=[
            pltpu.SemaphoreType.DMA((count,)),
            pltpu.SemaphoreType.DMA((count, bits + 1)),
            pltpu.SemaphoreType.DMA((count, bits + 1)),
        ],
        compiler_params=pltpu.CompilerParams(collective_id=1, has_side_effects=True),
        name="gather_weights",
    )(*shards)
    return [f.reshape((2, slabs * s.shape[0], s.shape[1])) for f, s in zip(full, shards)]


def beside(full):
    return jnp.concatenate([full[0], full[1]], axis=1)


def total_kernel(groups, in_ref, out_ref, *refs):
    count = len(groups)
    buffers = refs[:count]
    sends, recvs = refs[count:]
    place, core = lax.axis_index("dp"), lax.axis_index("tp")

    def digit(bit):
        return core if bit < 0 else (place // (1 << bit)) % 2

    def peer(group, flip):
        there, other = place, core
        for n, bit in enumerate(group):
            if flip & (1 << n):
                if bit < 0:
                    other = 1 - core
                else:
                    there = there + (1 - 2 * digit(bit)) * (1 << bit)
        return (there, other)

    barrier = pltpu.get_barrier_semaphore()
    signals = 0
    for group in groups:
        for flip in range(1, 1 << len(group)):
            pl.semaphore_signal(
                barrier, inc=1, device_id=peer(group, flip), device_id_type=MESH
            )
            signals += 1
    pl.semaphore_wait(barrier, signals)

    value = in_ref[...]
    sem, started = 0, []
    for group, buffer in zip(groups, buffers):
        mine = sum(digit(bit) * (1 << n) for n, bit in enumerate(group))
        buffer[mine] = value
        copies = []
        for flip in range(1, 1 << len(group)):
            copy = pltpu.make_async_remote_copy(
                src_ref=buffer.at[mine],
                dst_ref=buffer.at[mine],
                send_sem=sends.at[sem],
                recv_sem=recvs.at[sem],
                device_id=peer(group, flip),
                device_id_type=MESH,
            )
            copy.start()
            copies.append(copy)
            sem += 1
        for copy in copies:
            copy.wait_recv()
        started += copies
        value = buffer[0]
        for n in range(1, 1 << len(group)):
            value = value + buffer[n]
    out_ref[...] = value
    for copy in started:
        copy.wait_send()


def call_total(sums, n_dp):
    bits = n_dp.bit_length() - 1
    groups = [(-1, 0, 1)] + [tuple(range(b, min(b + 2, bits))) for b in range(2, bits, 2)]
    peers = sum((1 << len(g)) - 1 for g in groups)
    return pl.pallas_call(
        functools.partial(total_kernel, groups),
        out_shape=jax.ShapeDtypeStruct(sums.shape, sums.dtype),
        in_specs=[pl.BlockSpec(memory_space=pltpu.VMEM)],
        out_specs=pl.BlockSpec(memory_space=pltpu.VMEM),
        scratch_shapes=[pltpu.VMEM((1 << len(g),) + sums.shape, jnp.float32) for g in groups]
        + [pltpu.SemaphoreType.DMA((peers,)), pltpu.SemaphoreType.DMA((peers,))],
        compiler_params=pltpu.CompilerParams(collective_id=2, has_side_effects=True),
        name="total",
    )(sums)


SCORES, MIX, MIX_BACK = "qhe,khe->hqk", "hqk,khe->qhe", "hqk,qhe->khe"


def masked_scores(queries, keys, segments):
    raw = jnp.einsum(SCORES, queries, keys, preferred_element_type=jnp.float32)
    same = segments[:, None] == segments[None, :]
    return jnp.where(same[None, :, :], raw, MASKED)


def attend_forward(parts):
    queries, keys, values, segments = parts
    scores = masked_scores(queries, keys, segments)
    top = jnp.max(scores, axis=-1, keepdims=True)
    powers = jnp.exp(scores - top)
    total = jnp.sum(powers, axis=-1, keepdims=True)
    weights_low = (powers / total).astype(jnp.bfloat16)
    mixed = jnp.einsum(MIX, weights_low, values, preferred_element_type=jnp.float32)
    return mixed.astype(jnp.bfloat16), (top + jnp.log(total))[:, :, 0]


def attend_backward(parts):
    queries, keys, values, segments, logsum, mixed_grad = parts
    bf16, f32 = jnp.bfloat16, jnp.float32
    scores = masked_scores(queries, keys, segments)
    probs = jnp.exp(scores - logsum[:, :, None])
    value_grad = jnp.einsum(MIX_BACK, probs.astype(bf16), mixed_grad, preferred_element_type=f32)
    prob_grad = jnp.einsum(SCORES, mixed_grad, values, preferred_element_type=f32)
    total = jnp.sum(probs * prob_grad, axis=-1, keepdims=True)
    score_grad = (probs * (prob_grad - total)).astype(bf16)
    query_grad = jnp.einsum(MIX, score_grad, keys, preferred_element_type=f32)
    key_grad = jnp.einsum(MIX_BACK, score_grad, queries, preferred_element_type=f32)
    query_grad = query_grad * (1.0 / math.sqrt(HD))
    return query_grad.astype(bf16), key_grad.astype(bf16), value_grad.astype(bf16)


def whole_sequences(a, w):
    bf16 = jnp.bfloat16
    tokens, segments = a.tokens, a.segments
    rows, model = tokens.shape
    queries = (dot(tokens, w.query) * (1.0 / math.sqrt(HD))).astype(bf16)
    keys = dot(tokens, w.key).astype(bf16)
    values = dot(tokens, w.value).astype(bf16)
    split = (segments.shape[0], SEQ_LEN, model // HD, HD)
    blocks = [x.reshape(split) for x in (queries, keys, values)] + [segments]
    mixed, logsum = lax.map(attend_forward, tuple(blocks))
    attention = dot_nt(mixed.reshape(rows, model), w.out_t)
    normed_one, inverse_one = normalize(tokens.astype(jnp.float32) + attention)
    hidden = normed_one * a.gain_one
    branch, slopes = 0.0, []
    for w_in, ff_t in ((w.w_in, w.ff_t),):
        inner, back = jax.vjp(
            lambda x: jax.nn.gelu(x, approximate=False), dot(hidden.astype(bf16), w_in)
        )
        slopes.append(back)
        branch = branch + dot_nt(inner.astype(bf16), ff_t)
    normed_two, inverse_two = normalize(hidden + branch)
    output = (normed_two * a.gain_two).astype(bf16)
    grad = norm_back(a.cotangent.astype(jnp.float32) * a.gain_two, normed_two, inverse_two)
    low = grad.astype(bf16)
    for w_in, ff_t, back in ((w.w_in, w.ff_t, slopes[0]),):
        grad = grad + dot_nt(back(dot(low, ff_t))[0].astype(bf16), w_in)
    sum_one = norm_back(grad * a.gain_one, normed_one, inverse_one)
    mixed_grad = dot(sum_one.astype(bf16), w.out_t).astype(bf16)
    grads = lax.map(attend_backward, tuple(blocks) + (logsum, mixed_grad.reshape(split)))
    query_grad, key_grad, value_grad = [g.reshape(rows, model) for g in grads]
    token_grad = sum_one + dot_nt(query_grad, w.query) + dot_nt(key_grad, w.key)
    token_grad = token_grad + dot_nt(value_grad, w.value)
    low = dot(tokens, w.down).astype(bf16)
    sums = []
    for scale, bias, grad in (
        (a.query_scale, a.query_bias, query_grad),
        (a.value_scale, a.value_bias, value_grad),
    ):
        product = dot_tn(low, grad) * w.up.astype(jnp.float32)
        sums.append(jnp.sum(product * bias, axis=1))
        over = jnp.sum(product * scale[:, None], axis=0)
        sums.append(jnp.pad(over, (0, low.shape[1] - model)))
    return output, token_grad, jnp.stack(sums)


def call_layer(stride, bits, n_dp, a, rows):
    model = a.tokens.shape[1]
    slab, width = a.w_query.shape
    quarters = a.w_in.shape[1] // width
    ranks = a.down.shape[1]
    seqs, pairs = rows // SEQ_LEN, model // LANES
    bf16, f32 = jnp.bfloat16, jnp.float32
    lead = (2,) * bits
    square = lead + (slab, model)
    up_shape = lead + (a.up.shape[0], model)
    all_bits = n_dp.bit_length() - 1
    groups = [(-1, 0, 1)] + [tuple(range(b, min(b + 2, all_bits))) for b in range(2, all_bits, 2)]
    peers = sum((1 << len(g)) - 1 for g in groups)

    hbm = dict(
        tokens=a.tokens,
        cotangent=a.cotangent,
        w_key=a.w_key,
        out_t=a.out_t,
        w_in=a.w_in,
        ff_t=a.ff_t,
        up=a.up,
    )
    vmem = dict(
        segments=a.segments,
        w_query=a.w_query,
        w_value=a.w_value,
        down=a.down,
        gain_one=a.gain_one,
        gain_two=a.gain_two,
        query_scale=a.query_scale,
        query_bias=a.query_bias,
        value_scale=a.value_scale,
        value_bias=a.value_bias,
    )
    outs = dict(o_output=((rows, model), bf16), o_grad=((rows, model), f32))
    kept = dict(o_sums=((4, ranks), f32), o_flag=((1, 1), f32))
    scratch = dict(
        up_full=(up_shape, bf16),
        query_full=(square, bf16),
        key_full=(square, bf16),
        value_full=(square, bf16),
        out_full=(square, bf16),
        down_full=(lead + (slab, ranks), bf16),
        win=(lead + (slab, quarters * model), bf16),
        wout=(lead + (slab, quarters * model), bf16),
        query_own=((slab, width), bf16),
        value_own=((slab, width), bf16),
        raw=((rows, model), bf16),
        tok=((rows, model), bf16),
        turn=((seqs, SEQ_LEN, SEQ_LEN), bf16),
        same=((seqs, SPAN, SPAN), f32),
        lowest=((8, 2 * SPAN), f32),
        logsum=((2 * seqs, 8, 2 * SPAN), f32),
        queries=((rows, model), bf16),
        keys=((rows, model), bf16),
        values=((rows, model), bf16),
        mixed=((rows, model), bf16),
        normed=((rows, model), f32),
        inverse=((rows, LANES), f32),
        hidden=((rows, model), bf16),
        inner=((rows, quarters * model), bf16),
        slope=((rows, quarters * model), bf16),
        wide=((rows, model), f32),
        projected=((ranks, rows), bf16),
        sums=((4, ranks), f32),
    )
    sems = dict(
        own_sems=(len(PIECES),),
        send_sems=(len(PIECES), bits + 1),
        recv_sems=(len(PIECES), bits + 1),
        total_sends=(peers,),
        total_recvs=(peers,),
        in_sems=(2,),
        out_sems=(2, seqs),
    )
    names = tuple(hbm) + tuple(vmem) + tuple(outs) + tuple(kept) + tuple(scratch) + tuple(sems)
    results = pl.pallas_call(
        functools.partial(layer_kernel, stride, bits, groups, names),
        out_shape=[jax.ShapeDtypeStruct(*v) for v in (outs | kept).values()],
        in_specs=[pl.BlockSpec(memory_space=pl.ANY)] * len(hbm)
        + [pl.BlockSpec(memory_space=pltpu.VMEM)] * len(vmem),
        out_specs=[pl.BlockSpec(memory_space=pl.ANY)] * len(outs)
        + [pl.BlockSpec(memory_space=pltpu.VMEM)] * len(kept),
        scratch_shapes=[pltpu.VMEM(*v) for v in scratch.values()]
        + [pltpu.SemaphoreType.DMA(v) for v in sems.values()]
        + [pltpu.VMEM((1 << len(g), 4, ranks), f32) for g in groups],
        compiler_params=pltpu.CompilerParams(
            collective_id=0, has_side_effects=True, vmem_limit_bytes=VMEM_LIMIT
        ),
        name="layer",
    )(*hbm.values(), *vmem.values())
    return results


def call_hand(output, grad, sums):
    f32 = jnp.float32
    ranks, (rows, model) = sums.shape[1], grad.shape
    grad, output, *totals = pl.pallas_call(
        hand_kernel,
        out_shape=[
            jax.ShapeDtypeStruct(grad.shape, grad.dtype),
            jax.ShapeDtypeStruct(output.shape, output.dtype),
            jax.ShapeDtypeStruct((ranks,), f32),
            jax.ShapeDtypeStruct((model,), f32),
            jax.ShapeDtypeStruct((ranks,), f32),
            jax.ShapeDtypeStruct((model,), f32),
        ],
        in_specs=[pl.BlockSpec(memory_space=pl.ANY)] * 2 + [pl.BlockSpec(memory_space=pltpu.VMEM)],
        out_specs=[pl.BlockSpec(memory_space=pl.ANY)] * 2
        + [pl.BlockSpec(memory_space=pltpu.VMEM)] * 4,
        scratch_shapes=[
            pltpu.VMEM(grad.shape, grad.dtype),
            pltpu.VMEM(output.shape, output.dtype),
            pltpu.SemaphoreType.DMA((2, 2, COPIES)),
        ],
        compiler_params=pltpu.CompilerParams(vmem_limit_bytes=VMEM_LIMIT),
        name="hand",
    )(grad, output, sums)
    return (output, grad) + tuple(totals)


def per_device(
    n_dp,
    tokens,
    segment_ids,
    cotangent,
    w_query,
    w_key,
    w_value,
    w_output,
    shared_down,
    shared_up,
    w_in,
    w_out,
    gain_one,
    gain_two,
    query_scale,
    query_bias,
    value_scale,
    value_bias,
):
    rows, model = tokens.shape[0] // 2, tokens.shape[1]
    ranks = shared_down.shape[1]
    shards = dict(
        w_query=w_query,
        w_key=w_key,
        w_value=w_value,
        out_t=w_output.T,
        down=shared_down,
        up=shared_up,
        w_in=w_in,
        ff_t=w_out.T,
    )
    stride = n_dp // SLABS
    if stride > 1:
        groups = [list(range(g * stride, (g + 1) * stride)) for g in range(SLABS)]
        gather = functools.partial(lax.all_gather, axis=0, tiled=True, axis_index_groups=groups)
        shards = {n: gather(s, "dp") for n, s in shards.items()}
    arrays = types.SimpleNamespace(
        **shards,
        tokens=tokens,
        cotangent=cotangent,
        segments=segment_ids,
        gain_one=gain_one,
        gain_two=gain_two,
        query_scale=query_scale,
        query_bias=query_bias,
        value_scale=value_scale,
        value_bias=value_bias,
    )
    bits = SLABS.bit_length() - 1
    output, grad, sums, flag = call_layer(stride, bits, n_dp, arrays, rows)
    def halves():
        return call_hand(output, grad, sums)

    def whole():
        core = lax.axis_index("tp")
        own = types.SimpleNamespace(**vars(arrays))
        own.tokens = lax.dynamic_slice_in_dim(tokens, core * rows, rows, 0)
        own.cotangent = lax.dynamic_slice_in_dim(cotangent, core * rows, rows, 0)
        count = segment_ids.shape[0] // 2
        own.segments = lax.dynamic_slice_in_dim(segment_ids, core * count, count, 0)
        half = lax.dynamic_slice_in_dim(arrays.down, core * (ranks // 2), ranks // 2, 1)
        names = ("query", "key", "value", "out_t", "up", "down", "w_in", "ff_t")
        mine = [arrays.w_query, arrays.w_key, arrays.w_value, arrays.out_t, arrays.up, half]
        mine += [arrays.w_in, arrays.ff_t]
        order = tuple(range(bits - 1, -1, -1))
        full = gather_weights(mine, [order] * len(mine), SLABS, stride)
        full = [jnp.concatenate([f[0], f[1]], axis=1) for f in full]
        weights = types.SimpleNamespace(**dict(zip(names, full)))
        for scale, bias, name in (
            (query_scale, query_bias, "query"),
            (value_scale, value_bias, "value"),
        ):
            extra = dot((weights.down * scale).astype(jnp.bfloat16), weights.up) * bias
            setattr(weights, name, (getattr(weights, name) + extra).astype(jnp.bfloat16))
        output, token_grad, parts = whole_sequences(own, weights)
        return call_hand(output, token_grad, call_total(parts, n_dp))

    return lax.cond(flag[0, 0] == 0.0, halves, whole)


def solution(mesh):
    in_specs = (
        P("dp", None),
        P("dp", None),
        P("dp", None),
        P("dp", "tp"),
        P("dp", "tp"),
        P("dp", "tp"),
        P("tp", "dp"),
        P("dp", None),
        P("dp", "tp"),
        P("dp", "tp"),
        P("tp", "dp"),
        P(),
        P(),
        P(),
        P(),
        P(),
        P(),
    )
    out_specs = (P(("dp", "tp"), None), P(("dp", "tp"), None), P(), P(), P(), P())
    return jax.shard_map(
        functools.partial(per_device, mesh.shape["dp"]),
        mesh=mesh,
        in_specs=in_specs,
        out_specs=out_specs,
        check_vma=False,
    )
```

time: 418 us -> 140 us (0.33); the launches traced: 413 us -> 140 us
  matrix products: 159 us -> 0 us
  local copies, waits for them, and re-layouts: 90.2 us -> 0.05 us
  Pallas kernels: 90.4 us -> 138 us
  blocking collectives: 39.2 us -> 0 us
  other arithmetic: 31.9 us -> 0 us
    dot_general x31 -> x0, matrix products: 159 us -> none  [the longest x9 58.7 us: times_transposed(): lax.dot_general(left, right, (((1,), (1,)), ((), ())), preferred_element_...]
    pallas_call x1 -> x2, Pallas kernels: 90.4 us -> 138 us  [the longest x1 134 us: call_layer(): pl.pallas_call(functools.partial(layer_kernel, stride, bits, groups, name...]
    psum x1 -> x0, blocking collectives: 39.2 us -> none  [per_device(): lax.psum((query_scale_part, query_bias_part, value_scale_part, value_bias...]
    unnamed x182 -> x26, local copies, waits for them, and re-layouts: 34 us -> 0.05 us
    while x36 -> x0, local copies, waits for them, and re-layouts: 19.3 us -> none  [the longest x4 9.24 us: per_device(): lax.map(attend_forward, (query_blocks, key_blocks, value_blocks, segment_...]
    reduce_sum x7 -> x0, other arithmetic: 15.6 us -> none  [the longest x2 5.14 us: attend_forward(): total = jnp.sum(powers, axis=-1, keepdims=True)]
    convert_element_type x2 -> x0, other arithmetic: 14.2 us -> none  [attend_backward(): (probs * (prob_grad - jnp.sum(probs * prob_grad, axis=-1, keepdims=True))...]
    reshape x6 -> x0, local copies, waits for them, and re-layouts: 10.6 us -> none  [the longest x1 2.61 us: per_device(): query_grad = query_grad.reshape(rows, heads * HD)]
where the time goes in v2:
time: 140 us
  Pallas kernels  138 us (99%)
  between operations  1.76 us (1%)
    pallas_call x1, Pallas kernels, call_layer(): pl.pallas_call(functools.partial(layer_kernel, stride, bits, groups, name...  134 us
    pallas_call x1, Pallas kernels, call_hand(): pl.pallas_call(hand_kernel, out_shape=[jax.ShapeDtypeStruct(grad.shape, g...  4.45 us

profile of v2, /device:TPU:0, one launch (start us, length us, event | category | flops | bytes accessed | tf_op | source)
XLA Modules:
  0.0 140.3 jit_solution(13731391837751890476)
XLA Ops:
  0.6 0.0 copy-start.45
  0.6 0.0 copy-start.46
  0.7 0.0 copy-start.49
  0.7 0.0 copy-start.50
  0.7 0.0 copy-start.53
  0.7 0.0 copy-start.54
  0.7 0.0 copy-start.55
  0.7 0.0 copy-start.56
  0.7 0.0 copy-start.59
  0.7 0.0 copy-start.68
  0.7 0.0 copy-start.71
  0.7 0.0 copy-start.74
  0.8 0.0 copy-start.77
  0.8 133.7 %layer.1 = (bf16[1024,768]{1,0:T(8,128)(2,1)}, f32[1024,768]{1,0:T(8,128)}, f32[4,1024]{1,0:T(4,128)S(1)}, f32[1,1]{1,0:T(1,128)}) custom-call(bf16[2048,768]{1,0:T(8,128)(2,1)} %refs_0_.1, bf16[2048,768]{1,0:T(8,128)(2,1)} %refs_1_.1, bf16[48,384]{1,0:T(8,128)(2,1)} %refs_2_.1, bf16[48,384]{1,0:T(8,128)(2,1)} %bitcast.220, bf16[48,1536]{1,0:T(8,128)(2,1)} %refs_4_.1, ...), custom_call_target="tpu_custom_call" | custom-call | tf_op jit(solution)/shard_map/layer/pallas_call | solution.py:841
  135.2 0.0 copy-done.45
  135.2 0.0 copy-done.46
  135.2 0.0 copy-done.49
  135.2 0.0 copy-done.50
  135.2 0.0 copy-done.53
  135.2 0.0 copy-done.54
  135.2 0.0 copy-done.55
  135.2 0.0 copy-done.56
  135.3 0.0 copy-done.59
  135.3 0.0 copy-done.68
  135.3 0.0 copy-done.71
  135.3 0.0 copy-done.74
  135.3 0.0 copy-done.77
  135.3 4.8 %conditional.1 = (bf16[1024,768]{1,0:T(8,128)(2,1)}, f32[1024,768]{1,0:T(8,128)}, f32[1024]{0:T(1024)}, f32[768]{0:T(1024)}, f32[1024]{0:T(1024)}, /*index=5*/f32[768]{0:T(1024)}) conditional(s32[]{:T(128)} %bitcast.41, (bf16[2048,768]{1,0:T(8,128)(2,1)}, bf16[48,1024]{1,0:T(8,128)(2,1)S(1)}, bf16[48,384]{1,0:T(8,128)(2,1)S(1)}, ...), branch_computations={%region_0.20_spmd, %region_20.21_spmd} | conditional | flops 39517421568 | bytes 794799040 | solution.py:964
  135.6 4.5 %hand.3 = (f32[1024,768]{1,0:T(8,128)}, bf16[1024,768]{1,0:T(8,128)(2,1)}, f32[1024]{0:T(1024)}, f32[768]{0:T(1024)}, f32[1024]{0:T(1024)}, /*index=5*/f32[768]{0:T(1024)}) custom-call(f32[1024,768]{1,0:T(8,128)} %get-tuple-element.163.grad, bf16[1024,768]{1,0:T(8,128)(2,1)} %get-tuple-element.164.output, f32[4,1024]{1,0:T(4,128)S(1)} %get-tuple-element.165.sums), custom_call_target="tpu_custom_call" | custom-call | tf_op jit(solution)/shard_map/cond/branch_1_fun/hand/pallas_call | solution.py:862
Async XLA Ops:
  0.6 134.5 %copy-start.45 = (bf16[48,1536]{1,0:T(8,128)(2,1)S(1)}, bf16[48,1536]{1,0:T(8,128)(2,1)}, u32[]{:S(2)}) copy-start(bf16[48,1536]{1,0:T(8,128)(2,1)} %refs_4_.1) | copy-start | bytes 442372
  0.6 134.5 %copy-start.46 = (bf16[1536,48]{0,1:T(8,128)(2,1)S(1)}, bf16[1536,48]{0,1:T(8,128)(2,1)}, u32[]{:S(2)}) copy-start(bf16[1536,48]{0,1:T(8,128)(2,1)} %param.33) | copy-start | bytes 442372
  0.7 134.5 %copy-start.49 = (bf16[48,1024]{1,0:T(8,128)(2,1)S(1)}, bf16[48,1024]{1,0:T(8,128)(2,1)}, u32[]{:S(2)}) copy-start(bf16[48,1024]{1,0:T(8,128)(2,1)} %refs_10_.1) | copy-start | bytes 294916
  0.7 134.5 %copy-start.50 = (bf16[64,384]{1,0:T(8,128)(2,1)S(1)}, bf16[64,384]{1,0:T(8,128)(2,1)}, u32[]{:S(2)}) copy-start(bf16[64,384]{1,0:T(8,128)(2,1)} %refs_6_.1) | copy-start | bytes 147460
  0.7 134.5 %copy-start.53 = (bf16[48,384]{1,0:T(8,128)(2,1)S(1)}, bf16[48,384]{1,0:T(8,128)(2,1)}, u32[]{:S(2)}) copy-start(bf16[48,384]{1,0:T(8,128)(2,1)} %refs_2_.1) | copy-start | bytes 110596
  0.7 134.5 %copy-start.54 = (bf16[384,48]{0,1:T(8,128)(2,1)S(1)}, bf16[384,48]{0,1:T(8,128)(2,1)}, u32[]{:S(2)}) copy-start(bf16[384,48]{0,1:T(8,128)(2,1)} %param.29) | copy-start | bytes 110596
  0.7 134.5 %copy-start.55 = (bf16[48,384]{1,0:T(8,128)(2,1)S(1)}, bf16[48,384]{1,0:T(8,128)(2,1)}, u32[]{:S(2)}) copy-start(bf16[48,384]{1,0:T(8,128)(2,1)} %refs_8_.1) | copy-start | bytes 110596
  0.7 134.5 %copy-start.56 = (bf16[48,384]{1,0:T(8,128)(2,1)S(1)}, bf16[48,384]{1,0:T(8,128)(2,1)}, u32[]{:S(2)}) copy-start(bf16[48,384]{1,0:T(8,128)(2,1)} %refs_9_.1) | copy-start | bytes 110596
  0.7 134.5 %copy-start.59 = (s32[4,512]{1,0:T(4,128)S(1)}, s32[4,512]{1,0:T(4,128)}, u32[]{:S(2)}) copy-start(s32[4,512]{1,0:T(4,128)} %refs_7_.1) | copy-start | bytes 24580
  0.7 134.5 %copy-start.68 = (f32[1024]{0:T(1024)S(1)}, f32[1024]{0:T(1024)}, u32[]{:S(2)}) copy-start(f32[1024]{0:T(1024)} %refs_13_.1) | copy-start | bytes 12292
  0.7 134.5 %copy-start.71 = (f32[768]{0:T(1024)S(1)}, f32[768]{0:T(1024)}, u32[]{:S(2)}) copy-start(f32[768]{0:T(1024)} %refs_14_.1) | copy-start | bytes 9220
  0.7 134.5 %copy-start.74 = (f32[1024]{0:T(1024)S(1)}, f32[1024]{0:T(1024)}, u32[]{:S(2)}) copy-start(f32[1024]{0:T(1024)} %refs_15_.1) | copy-start | bytes 12292
  0.8 134.5 %copy-start.77 = (f32[768]{0:T(1024)S(1)}, f32[768]{0:T(1024)}, u32[]{:S(2)}) copy-start(f32[768]{0:T(1024)} %refs_16_.1) | copy-start | bytes 9220
